TPU v7x, 32 devices: a whole 2x2x4 slice. The times are simulated.
32 devices in a mesh: groups: 2 (over y), mx: 4 (over z), my: 4 (over x, core).
Axes of the slice: x: 2, y: 2, z: 4, core: 2. Of those that a mesh axis runs over, the one named last changes fastest.
Arguments:
- tokens: bfloat16 [2048, 8192], P(('groups', 'mx'), 'my'), parts along dimension 0, may hold values from -6 to 6
- w_gate: bfloat16 [8192, 26624], P('my', 'mx'), may hold values from -0.0625 to 0.0625
- w_up: bfloat16 [8192, 26624], P('my', 'mx'), may hold values from -0.0625 to 0.0625
- adapter_in: bfloat16 [8, 8192, 32], P(None, 'my'), may hold values from -0.0625 to 0.0625
- adapter_out: bfloat16 [8, 2, 16, 26624], P(None, None, None, 'mx'), may hold values from -0.75 to 0.75
- magnitude: float32 [8, 2, 26624], P(None, None, 'mx'), may hold values from 0.5 to 2
- partial_norms: float32 [4, 8, 2, 26624], P('my', None, None, 'mx'), may hold values from 0.06 to 2.8125, as said below
- block_tenant: int32 [16], P('groups'), parts along dimension 0, may hold values from 0 to 7
- block_rows: int32 [16], P('groups'), parts along dimension 0, may hold values from 1 to 128, 768 in all
Outputs:
- hidden: bfloat16 [2048, 26624], P('groups', ('mx', 'my')), parts along dimension 0
There are 2 independent parts, one for each index of `groups`. A program takes and returns all parts, laid end to end along the dimension named above; an argument that names none is the same for every part. Nothing has to cross between parts.
Inputs may be any that keep to these rules, and one draw needn't show every extreme that they name: `partial_norms`: positive.
All inputs are finite; a program needn't handle non-finite values.
Results may differ from a plain program's by a relative error of at most 0.0038.
Values may be sent and summed in bfloat16 or wider, within the bound.
No kernel may reach another device: no remote copies, remote signals or barrier semaphores. Data moves between devices by JAX's collectives and lax.ppermute only.
A program may use at most 384 MiB of HBM per device.

v0:
```python
import functools
import math

import jax
import jax.numpy as jnp
from jax import lax
from jax.experimental import pallas as pl
from jax.experimental.pallas import tpu as pltpu
from jax.sharding import PartitionSpec as P

RANK = 16
BLOCK_ROWS = 128
LIVE_ROWS = 768
STEP_DEPTH = 512
TILE = 512
VMEM_LIMIT = 66 * 10**6

SLOTS = tuple((distance, half) for distance in (0, -1, 1, -2, 2, -3, 3) for half in range(2))
CHUNKS = ((0, 256, 6), (256, 256, 10), (512, 256, 14))
ANY = pl.BlockSpec(memory_space=pl.ANY)
COST = pl.CostEstimate(flops=0, bytes_accessed=0, transcendentals=0)
LONG = pl.CostEstimate(flops=10**12, bytes_accessed=0, transcendentals=0)


def fill_table(table, ids, rows, tenants, mx_count):
    start = jnp.int32(0)
    for slot, (distance, half) in enumerate(SLOTS):
        source = ids[0] + distance
        valid = (source >= 0) & (source < mx_count)
        block = jnp.clip(source, 0, mx_count - 1) * 2 + half
        count = jnp.where(valid, rows[block], 0)
        table[0, slot] = start
        table[1, slot] = count
        table[2, slot] = tenants[block]
        table[3, slot] = jnp.where(valid, block, -1)
        start = start + count


def pack_kernel(mx_count, first, rows_out, slots, passed, ids, rows, tenants, *refs):
    token_refs, down_ref = refs[:slots // 2], refs[slots // 2]
    outs, scratch = refs[-9 - passed:-6], refs[-6:]
    x_ref, low_ref, pick_ref = outs[:3]
    table, buffer, down, acc, sems, down_sem = scratch
    fill_table(table, ids, rows, tenants, mx_count)

    def needed(source):
        start, count = table[0, 2 * source], table[1, 2 * source] + table[1, 2 * source + 1]
        return (count > 0) & (start < first + rows_out) & (start + count > first)

    for source in range(slots // 2):
        @pl.when(needed(source))
        def _():
            pltpu.make_async_copy(token_refs[source], buffer.at[source], sems.at[source]).start()

    down_copies = [
        pltpu.make_async_copy(
            down_ref.at[pl.ds((2 * place + side) * RANK, RANK)], down.at[pl.ds((8 * side + place) * RANK, RANK)],
            down_sem.at[side, place],
        )
        for side in range(2) for place in range(8)
    ]
    for copy in down_copies:
        copy.start()
    acc[...] = jnp.zeros_like(acc)

    @pl.loop(0, slots // 2)
    def _(source):
        @pl.when(needed(source))
        def _():
            pltpu.make_async_copy(buffer.at[source], buffer.at[source], sems.at[source]).wait()
            target = lax.broadcasted_iota(jnp.int32, (rows_out, 2 * BLOCK_ROWS), 0) + first
            place = lax.broadcasted_iota(jnp.int32, (rows_out, 2 * BLOCK_ROWS), 1)
            upper = place >= BLOCK_ROWS
            position = jnp.where(upper, place - BLOCK_ROWS, place)
            start = jnp.where(upper, table[0, 2 * source + 1], table[0, 2 * source])
            count = jnp.where(upper, table[1, 2 * source + 1], table[1, 2 * source])
            chosen = (position < count) & (target == position + start)
            acc[...] += jnp.dot(
                chosen.astype(jnp.bfloat16), buffer[source], preferred_element_type=jnp.float32
            )

    x_ref[...] = acc[...].astype(jnp.bfloat16)
    row = lax.broadcasted_iota(jnp.int32, (rows_out, 128), 0) + first

    def own(slot, tenant):
        start, count = table[0, slot], table[1, slot]
        return jnp.where((row >= start) & (row < start + count), table[2, slot], tenant)

    tenant = lax.fori_loop(0, slots, own, jnp.full((rows_out, 128), -1, jnp.int32))
    lane = lax.broadcasted_iota(jnp.int32, (rows_out, 128), 1)
    pick_ref[...] = ((lane % 8 == tenant) & (lane < 24)).astype(jnp.bfloat16)

    for copy in down_copies:
        copy.wait()
    low = lax.dot_general(x_ref[...], down[...], (((1,), (1,)), ((), ())), preferred_element_type=jnp.float32)
    for side in range(2):
        mine = jnp.where(lane // RANK == tenant, low[:, side * 128:(side + 1) * 128], 0.0)
        high = mine.astype(jnp.bfloat16)
        low_ref[side, :, 0:128] = high
        low_ref[side, :, 128:256] = (mine - high.astype(jnp.float32)).astype(jnp.bfloat16)


def pack_rows(mx_count, chunk, scalars, tokens, down, after=(), passed=(), cost=COST):
    first, rows_out, slots = chunk
    width = down.shape[1]
    outs = [
        jax.ShapeDtypeStruct((rows_out, width), jnp.bfloat16),
        jax.ShapeDtypeStruct((2, rows_out, 256), jnp.bfloat16),
        jax.ShapeDtypeStruct((rows_out, 128), jnp.bfloat16),
    ]
    out_specs = [
        pl.BlockSpec((rows_out, width), lambda i, *_: (0, 0)),
        pl.BlockSpec((2, rows_out, 256), lambda i, *_: (0, 0, 0)),
        pl.BlockSpec((rows_out, 128), lambda i, *_: (0, 0)),
    ] + [ANY] * len(passed)
    return pl.pallas_call(
        functools.partial(pack_kernel, mx_count, first, rows_out, slots, len(passed)),
        out_shape=outs + [jax.ShapeDtypeStruct(tokens[i].shape, tokens[i].dtype) for i in passed],
        grid_spec=pltpu.PrefetchScalarGridSpec(
            num_scalar_prefetch=3,
            grid=(1,),
            in_specs=[ANY] * (len(tokens) + 1 + len(after)),
            out_specs=out_specs,
            scratch_shapes=[
                pltpu.SMEM((4, len(SLOTS)), jnp.int32),
                pltpu.VMEM((slots // 2, 2 * BLOCK_ROWS, width), jnp.bfloat16),
                pltpu.VMEM(down.shape, jnp.bfloat16),
                pltpu.VMEM((rows_out, width), jnp.float32),
                pltpu.SemaphoreType.DMA((slots // 2,)),
                pltpu.SemaphoreType.DMA((2, 8)),
            ],
        ),
        input_output_aliases={3 + place: 3 + i for i, place in enumerate(passed)},
        compiler_params=pltpu.CompilerParams(vmem_limit_bytes=VMEM_LIMIT),
        cost_estimate=cost,
        name="pack_rows",
    )(*scalars, *tokens, down, *after)


def activate(gate, up):
    return (gate * (1.0 / (1.0 + jnp.exp(-gate))) * up).astype(jnp.bfloat16)


def dot_kernel(flip, counts, splits, term_counts, finished, narrow, ids, *refs):
    parts = len(counts)
    finish = finished > 0
    x_refs, low_refs, refs = refs[:parts], refs[parts:2 * parts], refs[2 * parts:]
    w_refs, up_ref, refs = refs[:2], refs[2], refs[3:]
    terms = len(term_counts)
    term_refs, refs = refs[:2 * terms], refs[2 * terms:]
    if finish:
        far_refs, refs = refs[:finished], refs[finished:]
        pick_refs, scale_ref, refs = refs[:finished], refs[finished], refs[finished + 1:]
    x, low, w, maps, term, acc, out, far, pick, scale, in_sem, w_sem, out_sem = refs[-13:]
    outs = refs[-13 - (2 if finish else max(1, 2 * len(splits))):-13]
    done = sum(counts[:finished])
    rows, depth = x.shape
    steps = depth // STEP_DEPTH
    left = pl.multiple_of((ids[1] ^ flip) * narrow, 128)
    tiles = [(at, min(TILE, narrow - at)) for at in range(0, narrow, TILE)]
    loads = []

    def load(source, target):
        copy = pltpu.make_async_copy(source, target, in_sem.at[len(loads)])
        copy.start()
        loads.append(copy)

    def piece(side, step):
        return pltpu.make_async_copy(
            w_refs[side].at[pl.ds(step * STEP_DEPTH, STEP_DEPTH), pl.ds(left, narrow)],
            w.at[side, step], w_sem.at[side, step],
        )

    def start_step(step):
        for side in range(2):
            piece(side, step).start()

    def stores(at, size, place):
        columns = pl.ds(at, size)
        if finish:
            pairs = [(out.at[0, :, columns], outs[0].at[:, columns])]
            pairs += [(acc.at[side, pl.ds(done, rows - done), columns], outs[1].at[side, :, columns]) for side in range(2)]
        elif not splits:
            pairs = [(out.at[side, :, columns], outs[0].at[side, :, columns]) for side in range(2)]
        else:
            pairs = []
            for side in range(2):
                row = 0
                for part, count in enumerate(splits):
                    target = outs[side * len(splits) + part].at[:, columns]
                    pairs.append((out.at[side, pl.ds(row, count), columns], target))
                    row += count
        return [
            pltpu.make_async_copy(source, target, out_sem.at[place, i]) for i, (source, target) in enumerate(pairs)
        ]

    row = 0
    for part, count in enumerate(counts):
        load(x_refs[part], x.at[pl.ds(row, count)])
        load(low_refs[part], low.at[:, pl.ds(row, count)])
        row += count
    for side in range(2):
        load(up_ref.at[:, side, :, pl.ds(left, narrow)], maps.at[side, 0])
    first_loads = len(loads)
    start_step(0)
    start_step(1)
    if terms:
        for side in range(2):
            row = 0
            for part, count in enumerate(term_counts):
                load(term_refs[2 * part + side], term.at[side, pl.ds(row, count)])
                row += count
    if finish:
        row = 0
        for part, count in enumerate(counts[:finished]):
            here = pl.ds(row, count)
            load(far_refs[part], far.at[:, here])
            load(pick_refs[part], pick.at[here])
            row += count
        load(scale_ref, scale)

    for copy in loads[:first_loads]:
        copy.wait()
    for side in range(2):
        maps[side, 1] = maps[side, 0]

    @pl.loop(0, 2)
    def _(side):
        acc[side] = jnp.dot(low[side], maps[side].reshape(256, narrow), preferred_element_type=jnp.float32)

    @pl.loop(0, steps - 1)
    def _(step):
        for side in range(2):
            piece(side, step).wait()

            @pl.when(step + 2 < steps)
            def _():
                piece(side, step + 2).start()

        depths = pl.ds(pl.multiple_of(step * STEP_DEPTH, STEP_DEPTH), STEP_DEPTH)

        @pl.loop(0, 2)
        def _(side):
            acc[side] += jnp.dot(x[:, depths], w[side, step], preferred_element_type=jnp.float32)

    for copy in loads[first_loads:]:
        copy.wait()
    for side in range(2):
        piece(side, steps - 1).wait()

    def last_step(at, size, place):
        columns = pl.ds(at, size)
        values = []
        for side in range(2):
            value = acc[side, :, columns] + jnp.dot(
                x[:, depth - STEP_DEPTH:], w[side, steps - 1, :, columns], preferred_element_type=jnp.float32
            )
            if terms:
                value += term[side, :, columns].astype(jnp.float32)
            if finish:
                acc[side, done:, columns] = value[done:]
                value = value[:done] + far[side, :, columns].astype(jnp.float32)
                value *= jnp.dot(pick[...], scale[side, :, columns], preferred_element_type=jnp.float32)
                values.append(value)
            else:
                out[side, :, columns] = value.astype(out.dtype)
        if finish:
            out[0, :, columns] = activate(*values)
        for copy in stores(at, size, place):
            copy.start()

    whole = narrow // TILE

    @pl.loop(0, whole)
    def _(place):
        last_step(pl.multiple_of(place * TILE, TILE), TILE, place)

    for place in range(whole, len(tiles)):
        last_step(*tiles[place], place)
    for place, (at, size) in enumerate(tiles):
        for copy in stores(at, size, place):
            copy.wait()


def dot_pair(chunks, weights, adapter_out, flip, narrow, ids, splits=(), terms=(), finish=None, after=()):
    xs, lows, picks = zip(*chunks)
    counts = tuple(x.shape[0] for x in xs)
    rows, depth = sum(counts), xs[0].shape[1]
    tenants = adapter_out.shape[0]
    term_counts = tuple(gate.shape[0] for gate, _ in terms)
    operands = [ids, *xs, *lows, *weights, adapter_out, *[array for pair in terms for array in pair]]
    finished = 0
    if finish is not None:
        finished = len(finish[0])
        done = sum(counts[:finished])
        operands += [*finish[0], *picks[:finished], finish[1]]
        out_shape = [
            jax.ShapeDtypeStruct((done, narrow), jnp.bfloat16),
            jax.ShapeDtypeStruct((2, rows - done, narrow), jnp.float32),
        ]
    elif splits:
        out_shape = [jax.ShapeDtypeStruct((count, narrow), jnp.bfloat16) for _ in range(2) for count in splits]
    else:
        out_shape = [jax.ShapeDtypeStruct((2, rows, narrow), jnp.bfloat16)]
    operands += list(after)
    few = (8, 128)
    steps = depth // STEP_DEPTH
    return pl.pallas_call(
        functools.partial(
            dot_kernel, flip, counts, splits, term_counts, finished, narrow
        ),
        out_shape=out_shape,
        grid_spec=pltpu.PrefetchScalarGridSpec(
            num_scalar_prefetch=1,
            grid=(1,),
            in_specs=[ANY] * (len(operands) - 1),
            out_specs=[ANY] * len(out_shape),
            scratch_shapes=[
                pltpu.VMEM((rows, depth), jnp.bfloat16),
                pltpu.VMEM((2, rows, 256), jnp.bfloat16),
                pltpu.VMEM((2, steps, STEP_DEPTH, narrow), jnp.bfloat16),
                pltpu.VMEM((2, 2, tenants, RANK, narrow), jnp.bfloat16),
                pltpu.VMEM((2, rows, narrow) if terms else few, jnp.bfloat16),
                pltpu.VMEM((2, rows, narrow), jnp.float32),
                pltpu.VMEM((1, done, narrow) if finished else (2, rows, narrow), jnp.bfloat16),
                pltpu.VMEM((2, done, narrow) if finished else few, jnp.bfloat16),
                pltpu.VMEM((done, 128) if finished else few, jnp.bfloat16),
                pltpu.VMEM((2, 128, narrow) if finished else few, jnp.bfloat16),
                pltpu.SemaphoreType.DMA((4 * len(xs) + 8,)),
                pltpu.SemaphoreType.DMA((2, steps)),
                pltpu.SemaphoreType.DMA((-(-narrow // TILE), 4)),
            ],
        ),
        compiler_params=pltpu.CompilerParams(vmem_limit_bytes=VMEM_LIMIT),
        cost_estimate=COST,
        name="finish_dots" if finished else "dot_pair",
    )(*operands)


def last_kernel(
    mx_count, first, ids, rows, tenants, sums_ref, far_ref, pick, scale, earlier_ref, out_ref, table, sums, far, held,
    tile_sem, held_sem,
):
    block = pl.program_id(0)
    tiles = far.shape[1] // BLOCK_ROWS

    def tile_copies(tile):
        here = pl.ds(pl.multiple_of(tile * BLOCK_ROWS, BLOCK_ROWS), BLOCK_ROWS)
        return [
            pltpu.make_async_copy(source.at[:, here], target.at[:, here], tile_sem.at[tile, i])
            for i, (source, target) in enumerate([(sums_ref, sums), (far_ref, far)])
        ]

    @pl.when(block == 0)
    def _():
        for tile in range(tiles):
            for copy in tile_copies(tile):
                copy.start()
        held_copy = pltpu.make_async_copy(earlier_ref, held.at[pl.ds(0, first)], held_sem)
        held_copy.start()
        fill_table(table, ids, rows, tenants, mx_count)
        held[LIVE_ROWS:, :] = jnp.zeros((BLOCK_ROWS, held.shape[1]), held.dtype)
        columns = held.shape[1]

        @pl.loop(0, tiles)
        def _(tile):
            for copy in tile_copies(tile):
                copy.wait()
            here = pl.ds(pl.multiple_of(tile * BLOCK_ROWS, BLOCK_ROWS), BLOCK_ROWS)
            there = pl.ds(pl.multiple_of(first + tile * BLOCK_ROWS, BLOCK_ROWS), BLOCK_ROWS)
            for left in range(0, columns, TILE):
                right = min(left + TILE, columns)
                pre = [
                    (sums[side, here, left:right] + far[side, here, left:right].astype(jnp.float32))
                    * jnp.dot(pick[here, :], scale[side, :, left:right], preferred_element_type=jnp.float32)
                    for side in range(2)
                ]
                held[there, left:right] = activate(*pre)

        held_copy.wait()

    def find(slot, start):
        return jnp.where(table[3, slot] == block, table[0, slot], start)

    start = lax.fori_loop(0, len(SLOTS), find, jnp.int32(0))
    count = rows[block]
    base = pl.multiple_of(jnp.minimum(start // BLOCK_ROWS * BLOCK_ROWS, LIVE_ROWS - BLOCK_ROWS), BLOCK_ROWS)
    shape = (BLOCK_ROWS, 2 * BLOCK_ROWS)
    position = lax.broadcasted_iota(jnp.int32, shape, 0)
    column = lax.broadcasted_iota(jnp.int32, shape, 1) + base
    chosen = (position < count) & (column == position + start)
    out_ref[...] = jnp.dot(
        chosen.astype(jnp.bfloat16), held[pl.ds(base, 2 * BLOCK_ROWS), :], preferred_element_type=jnp.float32
    ).astype(jnp.bfloat16)


def last_rows(mx_count, first, scalars, sums, far, pick, scale, earlier, blocks):
    narrow = far.shape[2]
    operands = (sums, far, pick, scale, earlier)
    return pl.pallas_call(
        functools.partial(last_kernel, mx_count, first),
        out_shape=jax.ShapeDtypeStruct((blocks * BLOCK_ROWS, narrow), jnp.bfloat16),
        grid_spec=pltpu.PrefetchScalarGridSpec(
            num_scalar_prefetch=3,
            grid=(blocks,),
            in_specs=[
                ANY, ANY,
                pl.BlockSpec(pick.shape, lambda i, *_: (0, 0)),
                pl.BlockSpec(scale.shape, lambda i, *_: (0, 0, 0)),
                ANY,
            ],
            out_specs=pl.BlockSpec((BLOCK_ROWS, narrow), lambda i, *_: (i, 0)),
            scratch_shapes=[
                pltpu.SMEM((4, len(SLOTS)), jnp.int32),
                pltpu.VMEM(sums.shape, sums.dtype),
                pltpu.VMEM(far.shape, far.dtype),
                pltpu.VMEM((LIVE_ROWS + BLOCK_ROWS, narrow), jnp.bfloat16),
                pltpu.SemaphoreType.DMA((far.shape[1] // BLOCK_ROWS, 2)),
                pltpu.SemaphoreType.DMA,
            ],
        ),
        compiler_params=pltpu.CompilerParams(vmem_limit_bytes=VMEM_LIMIT),
        cost_estimate=COST,
        name="last_rows",
    )(*scalars, *operands)


def quarter(array, index, narrow):
    return lax.dynamic_slice_in_dim(array, index * narrow, narrow, array.ndim - 1)


def pipelined(
    tokens, w_gate, w_up, adapter_in, adapter_out, magnitude, partial_norms, block_tenant, block_rows
):
    mx_count = lax.axis_size("mx")
    my_count = lax.axis_size("my")
    narrow = w_gate.shape[1] // my_count
    mine = lax.axis_index("my")
    ids = jnp.stack([lax.axis_index("mx"), mine]).astype(jnp.int32)
    scalars = (ids, block_rows, block_tenant)
    near = [(i, i ^ 1) for i in range(my_count)]
    across = [(i, i ^ 2) for i in range(my_count)]

    def hop(block, distance, least=0):
        if distance > 0:
            pairs = [(i, i + distance) for i in range(least, mx_count - distance)]
        else:
            pairs = [(i, i + distance) for i in range(-distance, mx_count - least)]
        return lax.ppermute(block, "mx", pairs)

    blocks = [tokens, hop(tokens, 1), hop(tokens, -1)]

    norms = partial_norms[0]
    pair = jnp.stack([quarter(norms, mine, narrow), quarter(norms, mine ^ 2, narrow)])
    other = jnp.stack([quarter(norms, mine ^ 1, narrow), quarter(norms, mine ^ 3, narrow)])
    pair = pair + lax.ppermute(other, "my", near)
    norm_total = pair[0] + lax.ppermute(pair[1], "my", across)
    scale = quarter(magnitude, mine, narrow) * lax.rsqrt(norm_total)
    scale = jnp.transpose(scale, (1, 0, 2))
    high = lax.reduce_precision(scale, 8, 7)
    middle = lax.reduce_precision(scale - high, 8, 7)
    rest = scale - high - middle
    scale = jnp.concatenate(
        [high, middle, rest, jnp.zeros((2, 128 - 3 * scale.shape[1], narrow), jnp.float32)], axis=1
    ).astype(jnp.bfloat16)

    down = jnp.transpose(adapter_in, (0, 2, 1)).reshape(-1, adapter_in.shape[1])

    dots = functools.partial(
        dot_pair, weights=(w_gate, w_up), adapter_out=adapter_out, narrow=narrow, ids=ids
    )

    def swap(parts, pairs):
        return [lax.ppermute(part, "my", pairs) for part in parts]

    def far_out(chunk, after=()):
        return dots([chunk], flip=3, splits=(chunk[0].shape[0],), after=after)

    def far_in(chunk, got, after=()):
        part, = dots([chunk], flip=2, terms=(got,), after=after)
        return part, lax.ppermute(part, "my", across)

    *chunk0, up, down_line = pack_rows(
        mx_count, CHUNKS[0], scalars, blocks, down, after=(scale,), passed=(1, 2)
    )
    blocks = [tokens, up, down_line, hop(up, 1, 1), hop(down_line, -1, 1)]
    mark, far0 = far_in(chunk0, swap(far_out(chunk0), near))

    third_hop = [hop(blocks[3], 1, 2), hop(blocks[4], -1, 2)]
    *chunk1, = pack_rows(mx_count, CHUNKS[1], scalars, blocks, down, after=(mark,), cost=LONG)
    blocks += third_hop
    mark, far1 = far_in(chunk1, swap(far_out(chunk1), near))

    first, last = CHUNKS[2][:2]
    *chunk2, = pack_rows(mx_count, CHUNKS[2], scalars, blocks, down, after=(mark,))
    parts = far_out(chunk2, (far0,))
    got = swap(parts, near)
    parts = dots([chunk0, chunk1], flip=1, splits=(first,), after=(parts[0],))
    early = swap(parts, near)
    mark, far2 = far_in(chunk2, got, after=(parts[0],))

    parts = dots([chunk2], flip=1, splits=(last,), after=(mark,))
    late = swap(parts, near)
    hidden, sums = dots([chunk0, chunk1, chunk2], flip=0, terms=(early, late), finish=((far0, far1), scale))
    return last_rows(mx_count, first, scalars, sums, far2, chunk2[2], scale, hidden, block_rows.shape[0])


def adapter_low(rows_piece, aligned_row_total, adapter_in, block_tenant):
    row_count = rows_piece.shape[0]
    seg_rows = math.gcd(math.gcd(row_count, BLOCK_ROWS), aligned_row_total)
    seg_count = row_count // seg_rows
    seg_block = jnp.arange(seg_count, dtype=jnp.int32) * seg_rows // BLOCK_ROWS
    tenant_tables = adapter_in[block_tenant[seg_block]]
    grouped = rows_piece.reshape(seg_count, seg_rows, rows_piece.shape[1])
    low_terms = jnp.einsum(
        "skd,sdr->skr", grouped, tenant_tables, preferred_element_type=jnp.float32
    )
    return low_terms.reshape(row_count, tenant_tables.shape[2])


def finish_plain(
    summed, reduced_rank_factor, norm_total, mag_cols, adapter_cols, first_row, block_tenant, block_rows
):
    row_count = summed.shape[0]
    col_count = summed.shape[2]
    seg_rows = math.gcd(row_count, BLOCK_ROWS)
    seg_count = row_count // seg_rows
    seg_block = (first_row + jnp.arange(seg_count, dtype=jnp.int32) * seg_rows) // BLOCK_ROWS
    tenants = block_tenant[seg_block]
    col_scale = mag_cols * lax.rsqrt(norm_total)
    seg_scale = col_scale[tenants]
    seg_tables = adapter_cols[tenants]
    low_pair = reduced_rank_factor.reshape(seg_count, seg_rows, 2, RANK)
    adapted = jnp.einsum(
        "skpr,sprc->skpc", low_pair, seg_tables, preferred_element_type=jnp.float32
    )
    pre_act = (summed.reshape(seg_count, seg_rows, 2, col_count) + adapted) * seg_scale[:, None]
    hidden = jax.nn.silu(pre_act[:, :, 0]) * pre_act[:, :, 1]
    offsets = (first_row + jnp.arange(row_count, dtype=jnp.int32)).reshape(
        seg_count, seg_rows
    ) % BLOCK_ROWS
    live_mask = offsets < block_rows[seg_block][:, None]
    hidden = jnp.where(live_mask[:, :, None], hidden, jnp.zeros_like(hidden))
    return hidden.reshape(row_count, col_count).astype(jnp.bfloat16)


def plain(
    tokens, w_gate, w_up, adapter_in, adapter_out, magnitude, partial_norms, block_tenant, block_rows
):
    local_rows = tokens.shape[0]
    col_local = w_gate.shape[1]
    my_count = lax.axis_size("my")
    device_position = lax.axis_index("my")
    rows_piece = lax.all_gather(tokens, "mx", axis=0, tiled=True)
    gate_part = jnp.dot(rows_piece, w_gate, preferred_element_type=jnp.float32)
    up_part = jnp.dot(rows_piece, w_up, preferred_element_type=jnp.float32)
    main_part = jnp.stack((gate_part, up_part), axis=1)
    low_terms = adapter_low(rows_piece, local_rows, adapter_in, block_tenant)
    reduced_rank_factor = lax.psum(low_terms, "my").astype(jnp.bfloat16)
    summed = lax.psum_scatter(main_part, "my", scatter_dimension=2, tiled=True)
    norm_total = lax.psum_scatter(partial_norms[0], "my", scatter_dimension=2, tiled=True)
    narrow = col_local // my_count
    mag_cols = lax.dynamic_slice_in_dim(magnitude, device_position * narrow, narrow, 2)
    adapter_cols = lax.dynamic_slice_in_dim(adapter_out, device_position * narrow, narrow, 3)
    return finish_plain(
        summed, reduced_rank_factor, norm_total, mag_cols, adapter_cols, 0, block_tenant, block_rows
    )


def on_device(tokens, w_gate, w_up, adapter_in, *rest):
    my_count = lax.axis_size("my")
    fits = (
        my_count == 4
        and lax.axis_size("mx") == 4
        and tokens.shape[0] == 2 * BLOCK_ROWS
        and adapter_in.shape[0] == 8
        and tokens.shape[1] % STEP_DEPTH == 0
        and tokens.shape[1] >= 2 * STEP_DEPTH
        and w_gate.shape[1] % (my_count * 128) == 0
    )
    return (pipelined if fits else plain)(tokens, w_gate, w_up, adapter_in, *rest)


def solution(mesh):
    return jax.shard_map(
        on_device,
        mesh=mesh,
        in_specs=(
            P(("groups", "mx"), "my"),
            P("my", "mx"),
            P("my", "mx"),
            P(None, "my", None),
            P(None, None, None, "mx"),
            P(None, None, "mx"),
            P("my", None, None, "mx"),
            P("groups"),
            P("groups"),
        ),
        out_specs=P("groups", ("mx", "my")),
        check_vma=False,
    )
```

profile of v0, /device:TPU:8, one launch (start us, length us, event | category | flops | bytes accessed | tf_op | source)
XLA Modules:
  0.0 190.3 jit_solution(12976506458985914663)
XLA Ops:
  0.0 2.0 %collective-permute-start.1 = (bf16[256,2048]{1,0:T(8,128)(2,1)}, bf16[256,2048]{1,0:T(8,128)(2,1)}, u32[]{:S(2)}, u32[]{:S(2)}) collective-permute-start(bf16[256,2048]{1,0:T(8,128)(2,1)} %refs_0_.5), channel_id=1, source_target_pairs={{4,0},{8,4},{12,8},{5,1},{9,5},{13,9},{6,2},{10,6},{14,10},{7,3},{... | collective-permute-start | bytes 3145736 | tf_op jit(solution)/shard_map/ppermute | solution.py:449
  2.1 3.9 %collective-permute-start = (bf16[256,2048]{1,0:T(8,128)(2,1)}, bf16[256,2048]{1,0:T(8,128)(2,1)}, u32[]{:S(2)}, u32[]{:S(2)}) collective-permute-start(bf16[256,2048]{1,0:T(8,128)(2,1)} %refs_0_.5), channel_id=1, source_target_pairs={{0,4},{4,8},{8,12},{1,5},{5,9},{9,13},{2,6},{6,10},{10,14},{3,7},{... | collective-permute-start | bytes 3145736 | tf_op jit(solution)/shard_map/ppermute | solution.py:449
  10.9 2.9 %collective-permute-done.3 = f32[8,2,1664]{2,0,1:T(8,128)S(1)} collective-permute-done((f32[8,2,1664]{2,0,1:T(8,128)S(1)}, f32[8,2,1664]{2,0,1:T(8,128)S(1)}, u32[]{:S(2)}, u32[]{:S(2)}) %collective-permute-start.3) | collective-permute-done | bytes 106528 | tf_op jit(solution)/shard_map/ppermute | solution.py:457
  14.9 12.3 %collective-permute-done.1.refs_2_ = bf16[256,2048]{1,0:T(8,128)(2,1)} collective-permute-done((bf16[256,2048]{1,0:T(8,128)(2,1)}, bf16[256,2048]{1,0:T(8,128)(2,1)}, u32[]{:S(2)}, u32[]{:S(2)}) %collective-permute-start.1) | collective-permute-done | bytes 1048608 | tf_op jit(solution)/shard_map/ppermute | solution.py:449
  27.2 1.9 %collective-permute-done.refs_1_ = bf16[256,2048]{1,0:T(8,128)(2,1)} collective-permute-done((bf16[256,2048]{1,0:T(8,128)(2,1)}, bf16[256,2048]{1,0:T(8,128)(2,1)}, u32[]{:S(2)}, u32[]{:S(2)}) %collective-permute-start) | collective-permute-done | bytes 1048608 | tf_op jit(solution)/shard_map/ppermute | solution.py:449
  29.2 4.6 %pack_rows.3 = (bf16[256,2048]{1,0:T(8,128)(2,1)}, bf16[2,256,256]{2,1,0:T(8,128)(2,1)}, bf16[256,128]{1,0:T(8,128)(2,1)}, bf16[256,2048]{1,0:T(8,128)(2,1)}, bf16[256,2048]{1,0:T(8,128)(2,1)}) custom-call(s32[2]{0:T(128)} %pad_add_fusion.ids, s32[8]{0:T(128)} %rows.7, s32[8]{0:T(128)} %tenants.7, ...), custom_call_target="tpu_custom_call", output_to_operand_aliasing={{3}: (4, {}), {4}: (5, {})} | custom-call | tf_op jit(solution)/shard_map/pack_rows/pallas_call | solution.py:116
  33.8 5.1 %collective-permute-start.4 = (bf16[256,2048]{1,0:T(8,128)(2,1)}, bf16[256,2048]{1,0:T(8,128)(2,1)}, u32[]{:S(2)}, u32[]{:S(2)}) collective-permute-start(bf16[256,2048]{1,0:T(8,128)(2,1)} %get-tuple-element.29.refs_1_), channel_id=1, source_target_pairs={{4,8},{8,12},{5,9},{9,13},{6,10},{10,14},{7,11},{11,15},{20,24},{2... | collective-permute-start | bytes 3145736 | tf_op jit(solution)/shard_map/ppermute | solution.py:449
  38.9 1.9 %collective-permute-start.5 = (bf16[256,2048]{1,0:T(8,128)(2,1)}, bf16[256,2048]{1,0:T(8,128)(2,1)}, u32[]{:S(2)}, u32[]{:S(2)}) collective-permute-start(bf16[256,2048]{1,0:T(8,128)(2,1)} %get-tuple-element.30.refs_2_), channel_id=1, source_target_pairs={{4,0},{8,4},{5,1},{9,5},{6,2},{10,6},{7,3},{11,7},{20,16},{24,20},... | collective-permute-start | bytes 3145736 | tf_op jit(solution)/shard_map/ppermute | solution.py:449
  40.8 9.8 %dot_pair.8 = (bf16[256,1664]{1,0:T(8,128)(2,1)}, bf16[256,1664]{1,0:T(8,128)(2,1)}) custom-call(s32[2]{0:T(128)} %pad_add_fusion.ids, bf16[256,2048]{1,0:T(8,128)(2,1)} %get-tuple-element.28.refs_0_, bf16[2,256,256]{2,1,0:T(8,128)(2,1)} %get-tuple-element.31.refs_1_.refs_2_.refs_3_, bf16[2048,6656]{1,0:T(8,128)(2,1)} %refs_6_.3, ...), custom_call_target="tpu_custom_call" | custom-call | tf_op jit(solution)/shard_map/dot_pair/pallas_call | solution.py:308
  51.2 2.2 %collective-permute-done.6.refs_5_ = bf16[256,1664]{1,0:T(8,128)(2,1)} collective-permute-done((bf16[256,1664]{1,0:T(8,128)(2,1)}, bf16[256,1664]{1,0:T(8,128)(2,1)}, u32[]{:S(2)}, u32[]{:S(2)}) %collective-permute-start.6) | collective-permute-done | bytes 852000 | tf_op jit(solution)/shard_map/ppermute | solution.py:474
  54.6 9.9 %dot_pair.9.refs_6_ = bf16[2,256,1664]{2,1,0:T(8,128)(2,1)} custom-call(s32[2]{0:T(128)} %pad_add_fusion.ids, bf16[256,2048]{1,0:T(8,128)(2,1)} %get-tuple-element.28.refs_0_, bf16[2,256,256]{2,1,0:T(8,128)(2,1)} %get-tuple-element.31.refs_1_.refs_2_.refs_3_, bf16[2048,6656]{1,0:T(8,128)(2,1)} %refs_6_.3, bf16[2048,6656]{1,0:T(8,128)(2,1)} %refs_7_.1, ...), custom_call_target="tpu_custom_call" | custom-call | tf_op jit(solution)/shard_map/dot_pair/pallas_call | solution.py:308
  67.8 2.2 %collective-permute-start.9 = (bf16[256,2048]{1,0:T(8,128)(2,1)}, bf16[256,2048]{1,0:T(8,128)(2,1)}, u32[]{:S(2)}, u32[]{:S(2)}) collective-permute-start(bf16[256,2048]{1,0:T(8,128)(2,1)} %collective-permute-done.5.refs_4_), channel_id=1, source_target_pairs={{4,0},{5,1},{6,2},{7,3},{20,16},{21,17},{22,18},{23,19}} | collective-permute-start | bytes 3145736 | tf_op jit(solution)/shard_map/ppermute | solution.py:449
  70.1 5.1 %pack_rows.4 = (bf16[256,2048]{1,0:T(8,128)(2,1)}, bf16[2,256,256]{2,1,0:T(8,128)(2,1)}, bf16[256,128]{1,0:T(8,128)(2,1)}) custom-call(s32[2]{0:T(128)} %pad_add_fusion.ids, s32[8]{0:T(128)} %rows.7, s32[8]{0:T(128)} %tenants.7, bf16[256,2048]{1,0:T(8,128)(2,1)} %refs_0_.5, bf16[256,2048]{1,0:T(8,128)(2,1)} %get-tuple-element.29.refs_1_, ...), custom_call_target="tpu_custom_call" | custom-call | flops 999999995904 | tf_op jit(solution)/shard_map/pack_rows/pallas_call | solution.py:116
  75.1 9.8 %dot_pair.10 = (bf16[256,1664]{1,0:T(8,128)(2,1)}, bf16[256,1664]{1,0:T(8,128)(2,1)}) custom-call(s32[2]{0:T(128)} %pad_add_fusion.ids, bf16[256,2048]{1,0:T(8,128)(2,1)} %get-tuple-element.34.refs_0_.refs_1_, bf16[2,256,256]{2,1,0:T(8,128)(2,1)} %get-tuple-element.35.refs_1_.refs_3_.refs_4_, bf16[2048,6656]{1,0:T(8,128)(2,1)} %refs_6_.3, ...), custom_call_target="tpu_custom_call" | custom-call | tf_op jit(solution)/shard_map/dot_pair/pallas_call | solution.py:308
  85.5 2.2 %collective-permute-done.10.refs_5_ = bf16[256,1664]{1,0:T(8,128)(2,1)} collective-permute-done((bf16[256,1664]{1,0:T(8,128)(2,1)}, bf16[256,1664]{1,0:T(8,128)(2,1)}, u32[]{:S(2)}, u32[]{:S(2)}) %collective-permute-start.10) | collective-permute-done | bytes 852000 | tf_op jit(solution)/shard_map/ppermute | solution.py:474
  89.0 9.9 %dot_pair.11.refs_8_ = bf16[2,256,1664]{2,1,0:T(8,128)(2,1)} custom-call(s32[2]{0:T(128)} %pad_add_fusion.ids, bf16[256,2048]{1,0:T(8,128)(2,1)} %get-tuple-element.34.refs_0_.refs_1_, bf16[2,256,256]{2,1,0:T(8,128)(2,1)} %get-tuple-element.35.refs_1_.refs_3_.refs_4_, bf16[2048,6656]{1,0:T(8,128)(2,1)} %refs_6_.3, bf16[2048,6656]{1,0:T(8,128)(2,1)} %refs_7_.1, ...), custom_call_target="tpu_custom_call" | custom-call | tf_op jit(solution)/shard_map/dot_pair/pallas_call | solution.py:308
  99.5 5.2 %pack_rows.5 = (bf16[256,2048]{1,0:T(8,128)(2,1)}, bf16[2,256,256]{2,1,0:T(8,128)(2,1)}, bf16[256,128]{1,0:T(8,128)(2,1)}) custom-call(s32[2]{0:T(128)} %pad_add_fusion.ids, s32[8]{0:T(128)} %rows.7, s32[8]{0:T(128)} %tenants.7, bf16[256,2048]{1,0:T(8,128)(2,1)} %refs_0_.5, bf16[256,2048]{1,0:T(8,128)(2,1)} %get-tuple-element.29.refs_1_, ...), custom_call_target="tpu_custom_call" | custom-call | tf_op jit(solution)/shard_map/pack_rows/pallas_call | solution.py:116
  105.0 9.8 %dot_pair.12 = (bf16[256,1664]{1,0:T(8,128)(2,1)}, bf16[256,1664]{1,0:T(8,128)(2,1)}) custom-call(s32[2]{0:T(128)} %pad_add_fusion.ids, bf16[256,2048]{1,0:T(8,128)(2,1)} %get-tuple-element.38.refs_0_.refs_2_, bf16[2,256,256]{2,1,0:T(8,128)(2,1)} %get-tuple-element.39.refs_1_.refs_5_, bf16[2048,6656]{1,0:T(8,128)(2,1)} %refs_6_.3, ...), custom_call_target="tpu_custom_call" | custom-call | tf_op jit(solution)/shard_map/dot_pair/pallas_call | solution.py:308
  115.4 14.4 %dot_pair.13 = (bf16[512,1664]{1,0:T(8,128)(2,1)}, bf16[512,1664]{1,0:T(8,128)(2,1)}) custom-call(s32[2]{0:T(128)} %pad_add_fusion.ids, bf16[256,2048]{1,0:T(8,128)(2,1)} %get-tuple-element.28.refs_0_, bf16[256,2048]{1,0:T(8,128)(2,1)} %get-tuple-element.34.refs_0_.refs_1_, bf16[2,256,256]{2,1,0:T(8,128)(2,1)} %get-tuple-element.31.refs_1_.refs_2_.refs_3_, ...), custom_call_target="tpu_custom_call" | custom-call | tf_op jit(solution)/shard_map/dot_pair/pallas_call | solution.py:308
  130.3 9.9 %dot_pair.14.refs_5_ = bf16[2,256,1664]{2,1,0:T(8,128)(2,1)} custom-call(s32[2]{0:T(128)} %pad_add_fusion.ids, bf16[256,2048]{1,0:T(8,128)(2,1)} %get-tuple-element.38.refs_0_.refs_2_, bf16[2,256,256]{2,1,0:T(8,128)(2,1)} %get-tuple-element.39.refs_1_.refs_5_, bf16[2048,6656]{1,0:T(8,128)(2,1)} %refs_6_.3, bf16[2048,6656]{1,0:T(8,128)(2,1)} %refs_7_.1, ...), custom_call_target="tpu_custom_call" | custom-call | tf_op jit(solution)/shard_map/dot_pair/pallas_call | solution.py:308
  141.8 10.1 %dot_pair.15 = (bf16[256,1664]{1,0:T(8,128)(2,1)}, bf16[256,1664]{1,0:T(8,128)(2,1)}) custom-call(s32[2]{0:T(128)} %pad_add_fusion.ids, bf16[256,2048]{1,0:T(8,128)(2,1)} %get-tuple-element.38.refs_0_.refs_2_, bf16[2,256,256]{2,1,0:T(8,128)(2,1)} %get-tuple-element.39.refs_1_.refs_5_, bf16[2048,6656]{1,0:T(8,128)(2,1)} %refs_6_.3, ...), custom_call_target="tpu_custom_call" | custom-call | tf_op jit(solution)/shard_map/dot_pair/pallas_call | solution.py:308
  152.4 2.2 %collective-permute-done.17.refs_11_ = bf16[256,1664]{1,0:T(8,128)(2,1)} collective-permute-done((bf16[256,1664]{1,0:T(8,128)(2,1)}, bf16[256,1664]{1,0:T(8,128)(2,1)}, u32[]{:S(2)}, u32[]{:S(2)}) %collective-permute-start.17) | collective-permute-done | bytes 852000 | tf_op jit(solution)/shard_map/ppermute | solution.py:474
  155.9 22.9 %finish_dots.1 = (bf16[512,1664]{1,0:T(8,128)(2,1)}, f32[2,256,1664]{2,1,0:T(8,128)}) custom-call(s32[2]{0:T(128)} %pad_add_fusion.ids, bf16[256,2048]{1,0:T(8,128)(2,1)} %get-tuple-element.28.refs_0_, bf16[256,2048]{1,0:T(8,128)(2,1)} %get-tuple-element.34.refs_0_.refs_1_, bf16[256,2048]{1,0:T(8,128)(2,1)} %get-tuple-element.38.refs_0_.refs_2_, ...), custom_call_target="tpu_custom_call" | custom-call | tf_op jit(solution)/shard_map/finish_dots/pallas_call | solution.py:308
  179.8 10.3 %last_rows.1 = bf16[1024,1664]{1,0:T(8,128)(2,1)} custom-call(s32[2]{0:T(128)} %pad_add_fusion.ids, s32[8]{0:T(128)} %rows.7, s32[8]{0:T(128)} %tenants.7, f32[2,256,1664]{2,1,0:T(8,128)} %get-tuple-element.48.sums_ref, bf16[2,256,1664]{2,1,0:T(8,128)(2,1)} %collective-permute-done.20.far_ref, bf16[256,128]{1,0:T(8,128)(2,1)} %get-tuple-element.49.pick, ...), custom_call_target="tpu_custom_call" | custom-call | tf_op jit(solution)/shard_map/last_rows/pallas_call | solution.py:400
  (50 shorter events, 19.1 us)
Async XLA Ops:
  0.0 7.4 %copy-start = (f32[8,2,6656]{2,1,0:T(2,128)S(1)}, f32[8,2,6656]{2,1,0:T(2,128)}, u32[]{:S(2)}) copy-start(f32[8,2,6656]{2,1,0:T(2,128)} %param.14) | copy-start | bytes 1277956
  0.0 27.2 %collective-permute-start.1 = (bf16[256,2048]{1,0:T(8,128)(2,1)}, bf16[256,2048]{1,0:T(8,128)(2,1)}, u32[]{:S(2)}, u32[]{:S(2)}) collective-permute-start(bf16[256,2048]{1,0:T(8,128)(2,1)} %refs_0_.5), channel_id=1, source_target_pairs={{4,0},{8,4},{12,8},{5,1},{9,5},{13,9},{6,2},{10,6},{14,10},{7,3},{... | collective-permute-start | bytes 3145736 | tf_op jit(solution)/shard_map/ppermute | solution.py:449
  2.1 27.1 %collective-permute-start = (bf16[256,2048]{1,0:T(8,128)(2,1)}, bf16[256,2048]{1,0:T(8,128)(2,1)}, u32[]{:S(2)}, u32[]{:S(2)}) collective-permute-start(bf16[256,2048]{1,0:T(8,128)(2,1)} %refs_0_.5), channel_id=1, source_target_pairs={{0,4},{4,8},{8,12},{1,5},{5,9},{9,13},{2,6},{6,10},{10,14},{3,7},{... | collective-permute-start | bytes 3145736 | tf_op jit(solution)/shard_map/ppermute | solution.py:449
  7.2 1.5 collective-permute-start.2
  8.8 5.1 %collective-permute-start.3 = (f32[8,2,1664]{2,0,1:T(8,128)S(1)}, f32[8,2,1664]{2,0,1:T(8,128)S(1)}, u32[]{:S(2)}, u32[]{:S(2)}) collective-permute-start(f32[8,2,1664]{2,0,1:T(8,128)S(1)} %slice_bitcast_fusion), channel_id=1, source_target_pairs={{0,2},{1,3},{2,0},{3,1},{4,6},{5,7},{6,4},{7,5},{8,10},{9,11},{10,... | collective-permute-start | bytes 319496 | tf_op jit(solution)/shard_map/ppermute | solution.py:457
  33.8 32.3 %collective-permute-start.4 = (bf16[256,2048]{1,0:T(8,128)(2,1)}, bf16[256,2048]{1,0:T(8,128)(2,1)}, u32[]{:S(2)}, u32[]{:S(2)}) collective-permute-start(bf16[256,2048]{1,0:T(8,128)(2,1)} %get-tuple-element.29.refs_1_), channel_id=1, source_target_pairs={{4,8},{8,12},{5,9},{9,13},{6,10},{10,14},{7,11},{11,15},{20,24},{2... | collective-permute-start | bytes 3145736 | tf_op jit(solution)/shard_map/ppermute | solution.py:449
  38.9 28.9 %collective-permute-start.5 = (bf16[256,2048]{1,0:T(8,128)(2,1)}, bf16[256,2048]{1,0:T(8,128)(2,1)}, u32[]{:S(2)}, u32[]{:S(2)}) collective-permute-start(bf16[256,2048]{1,0:T(8,128)(2,1)} %get-tuple-element.30.refs_2_), channel_id=1, source_target_pairs={{4,0},{8,4},{5,1},{9,5},{6,2},{10,6},{7,3},{11,7},{20,16},{24,20},... | collective-permute-start | bytes 3145736 | tf_op jit(solution)/shard_map/ppermute | solution.py:449
  50.6 2.8 %collective-permute-start.6 = (bf16[256,1664]{1,0:T(8,128)(2,1)}, bf16[256,1664]{1,0:T(8,128)(2,1)}, u32[]{:S(2)}, u32[]{:S(2)}) collective-permute-start(bf16[256,1664]{1,0:T(8,128)(2,1)} %get-tuple-element.32), channel_id=1, source_target_pairs={{0,1},{1,0},{2,3},{3,2},{4,5},{5,4},{6,7},{7,6},{8,9},{9,8},{10,11... | collective-permute-start | bytes 2555912 | tf_op jit(solution)/shard_map/ppermute | solution.py:474
  50.7 3.9 %collective-permute-start.7 = (bf16[256,1664]{1,0:T(8,128)(2,1)}, bf16[256,1664]{1,0:T(8,128)(2,1)}, u32[]{:S(2)}, u32[]{:S(2)}) collective-permute-start(bf16[256,1664]{1,0:T(8,128)(2,1)} %get-tuple-element.33), channel_id=1, source_target_pairs={{0,1},{1,0},{2,3},{3,2},{4,5},{5,4},{6,7},{7,6},{8,9},{9,8},{10,11... | collective-permute-start | bytes 2555912 | tf_op jit(solution)/shard_map/ppermute | solution.py:474
  64.6 40.4 %collective-permute-start.12 = (bf16[2,256,1664]{2,1,0:T(8,128)(2,1)}, bf16[2,256,1664]{2,1,0:T(8,128)(2,1)}, u32[]{:S(2)}, u32[]{:S(2)}) collective-permute-start(bf16[2,256,1664]{2,1,0:T(8,128)(2,1)} %dot_pair.9.refs_6_), channel_id=1, source_target_pairs={{0,2},{1,3},{2,0},{3,1},{4,6},{5,7},{6,4},{7,5},{8,10},{9,11},{10,... | collective-permute-start | bytes 5111816 | tf_op jit(solution)/shard_map/ppermute | solution.py:481
  66.1 33.4 %collective-permute-start.8 = (bf16[256,2048]{1,0:T(8,128)(2,1)}, bf16[256,2048]{1,0:T(8,128)(2,1)}, u32[]{:S(2)}, u32[]{:S(2)}) collective-permute-start(bf16[256,2048]{1,0:T(8,128)(2,1)} %collective-permute-done.4.refs_3_), channel_id=1, source_target_pairs={{8,12},{9,13},{10,14},{11,15},{24,28},{25,29},{26,30},{27,31}} | collective-permute-start | bytes 3145736 | tf_op jit(solution)/shard_map/ppermute | solution.py:449
  67.8 31.7 %collective-permute-start.9 = (bf16[256,2048]{1,0:T(8,128)(2,1)}, bf16[256,2048]{1,0:T(8,128)(2,1)}, u32[]{:S(2)}, u32[]{:S(2)}) collective-permute-start(bf16[256,2048]{1,0:T(8,128)(2,1)} %collective-permute-done.5.refs_4_), channel_id=1, source_target_pairs={{4,0},{5,1},{6,2},{7,3},{20,16},{21,17},{22,18},{23,19}} | collective-permute-start | bytes 3145736 | tf_op jit(solution)/shard_map/ppermute | solution.py:449
  85.0 2.8 %collective-permute-start.10 = (bf16[256,1664]{1,0:T(8,128)(2,1)}, bf16[256,1664]{1,0:T(8,128)(2,1)}, u32[]{:S(2)}, u32[]{:S(2)}) collective-permute-start(bf16[256,1664]{1,0:T(8,128)(2,1)} %get-tuple-element.36), channel_id=1, source_target_pairs={{0,1},{1,0},{2,3},{3,2},{4,5},{5,4},{6,7},{7,6},{8,9},{9,8},{10,11... | collective-permute-start | bytes 2555912 | tf_op jit(solution)/shard_map/ppermute | solution.py:474
  85.1 3.9 %collective-permute-start.11 = (bf16[256,1664]{1,0:T(8,128)(2,1)}, bf16[256,1664]{1,0:T(8,128)(2,1)}, u32[]{:S(2)}, u32[]{:S(2)}) collective-permute-start(bf16[256,1664]{1,0:T(8,128)(2,1)} %get-tuple-element.37), channel_id=1, source_target_pairs={{0,1},{1,0},{2,3},{3,2},{4,5},{5,4},{6,7},{7,6},{8,9},{9,8},{10,11... | collective-permute-start | bytes 2555912 | tf_op jit(solution)/shard_map/ppermute | solution.py:474
  98.9 53.0 %collective-permute-start.19 = (bf16[2,256,1664]{2,1,0:T(8,128)(2,1)}, bf16[2,256,1664]{2,1,0:T(8,128)(2,1)}, u32[]{:S(2)}, u32[]{:S(2)}) collective-permute-start(bf16[2,256,1664]{2,1,0:T(8,128)(2,1)} %dot_pair.11.refs_8_), channel_id=1, source_target_pairs={{0,2},{1,3},{2,0},{3,1},{4,6},{5,7},{6,4},{7,5},{8,10},{9,11},{10,... | collective-permute-start | bytes 5111816 | tf_op jit(solution)/shard_map/ppermute | solution.py:481
  114.8 15.5 %collective-permute-start.16 = (bf16[256,1664]{1,0:T(8,128)(2,1)}, bf16[256,1664]{1,0:T(8,128)(2,1)}, u32[]{:S(2)}, u32[]{:S(2)}) collective-permute-start(bf16[256,1664]{1,0:T(8,128)(2,1)} %get-tuple-element.43), channel_id=1, source_target_pairs={{0,1},{1,0},{2,3},{3,2},{4,5},{5,4},{6,7},{7,6},{8,9},{9,8},{10,11... | collective-permute-start | bytes 2555912 | tf_op jit(solution)/shard_map/ppermute | solution.py:474
  114.9 15.4 %collective-permute-start.15 = (bf16[256,1664]{1,0:T(8,128)(2,1)}, bf16[256,1664]{1,0:T(8,128)(2,1)}, u32[]{:S(2)}, u32[]{:S(2)}) collective-permute-start(bf16[256,1664]{1,0:T(8,128)(2,1)} %get-tuple-element.40.refs_7_), channel_id=1, source_target_pairs={{0,1},{1,0},{2,3},{3,2},{4,5},{5,4},{6,7},{7,6},{8,9},{9,8},{10,11... | collective-permute-start | bytes 2555912 | tf_op jit(solution)/shard_map/ppermute | solution.py:474
  129.8 26.1 %collective-permute-start.14 = (bf16[512,1664]{1,0:T(8,128)(2,1)}, bf16[512,1664]{1,0:T(8,128)(2,1)}, u32[]{:S(2)}, u32[]{:S(2)}) collective-permute-start(bf16[512,1664]{1,0:T(8,128)(2,1)} %get-tuple-element.42), channel_id=1, source_target_pairs={{0,1},{1,0},{2,3},{3,2},{4,5},{5,4},{6,7},{7,6},{8,9},{9,8},{10,11... | collective-permute-start | bytes 5111816 | tf_op jit(solution)/shard_map/ppermute | solution.py:474
  129.9 25.9 %collective-permute-start.13 = (bf16[512,1664]{1,0:T(8,128)(2,1)}, bf16[512,1664]{1,0:T(8,128)(2,1)}, u32[]{:S(2)}, u32[]{:S(2)}) collective-permute-start(bf16[512,1664]{1,0:T(8,128)(2,1)} %get-tuple-element.41.refs_7_), channel_id=1, source_target_pairs={{0,1},{1,0},{2,3},{3,2},{4,5},{5,4},{6,7},{7,6},{8,9},{9,8},{10,11... | collective-permute-start | bytes 5111816 | tf_op jit(solution)/shard_map/ppermute | solution.py:474
  140.3 39.5 %collective-permute-start.20 = (bf16[2,256,1664]{2,1,0:T(8,128)(2,1)}, bf16[2,256,1664]{2,1,0:T(8,128)(2,1)}, u32[]{:S(2)}, u32[]{:S(2)}) collective-permute-start(bf16[2,256,1664]{2,1,0:T(8,128)(2,1)} %dot_pair.14.refs_5_), channel_id=1, source_target_pairs={{0,2},{1,3},{2,0},{3,1},{4,6},{5,7},{6,4},{7,5},{8,10},{9,11},{10,... | collective-permute-start | bytes 5111816 | tf_op jit(solution)/shard_map/ppermute | solution.py:481
  151.8 2.8 %collective-permute-start.17 = (bf16[256,1664]{1,0:T(8,128)(2,1)}, bf16[256,1664]{1,0:T(8,128)(2,1)}, u32[]{:S(2)}, u32[]{:S(2)}) collective-permute-start(bf16[256,1664]{1,0:T(8,128)(2,1)} %get-tuple-element.44), channel_id=1, source_target_pairs={{0,1},{1,0},{2,3},{3,2},{4,5},{5,4},{6,7},{7,6},{8,9},{9,8},{10,11... | collective-permute-start | bytes 2555912 | tf_op jit(solution)/shard_map/ppermute | solution.py:474
  151.9 3.9 %collective-permute-start.18 = (bf16[256,1664]{1,0:T(8,128)(2,1)}, bf16[256,1664]{1,0:T(8,128)(2,1)}, u32[]{:S(2)}, u32[]{:S(2)}) collective-permute-start(bf16[256,1664]{1,0:T(8,128)(2,1)} %get-tuple-element.45), channel_id=1, source_target_pairs={{0,1},{1,0},{2,3},{3,2},{4,5},{5,4},{6,7},{7,6},{8,9},{9,8},{10,11... | collective-permute-start | bytes 2555912 | tf_op jit(solution)/shard_map/ppermute | solution.py:474
  179.8 10.3 %copy-start.1 = (f32[8,2,6656]{2,1,0:T(2,128)S(1)}, f32[8,2,6656]{2,1,0:T(2,128)}, u32[]{:S(2)}) copy-start(f32[8,2,6656]{2,1,0:T(2,128)} %param.14) | copy-start | bytes 1277956
where the time goes:
time: 192 us; the launch traced here: 190 us
  Pallas kernels  132 us (69%)
  waiting for transfers between devices  30 us (16%)
  starting transfers between devices  25.1 us (13%)
    pallas_call x9, Pallas kernels, dot_pair(): pl.pallas_call(functools.partial(dot_kernel, flip, counts, splits, term_c...  107 us
    ppermute x6, starting transfers between devices, hop(): return lax.ppermute(block, 'mx', pairs)  17 us
    pallas_call x3, Pallas kernels, pack_rows(): pl.pallas_call(functools.partial(pack_kernel, mx_count, first, rows_out,...  14.9 us
    ppermute x6, waiting for transfers between devices, hop(): return lax.ppermute(block, 'mx', pairs)  14.2 us
    pallas_call x1, Pallas kernels, last_rows(): pl.pallas_call(functools.partial(last_kernel, mx_count, first), out_shape...  10.3 us
    ppermute x10, waiting for transfers between devices, swap(): return [lax.ppermute(part, 'my', pairs) for part in parts]  10.3 us
  transfers between devices with their start and end apart: 21, of which 12 were waited for; matrix products, arithmetic and copies ran while one was open for 2% of the time, Pallas kernels for 61%

commit v1 on v0

--- a/solution.py
+++ b/solution.py
@@ -138,7 +138,8 @@
 
 
 def activate(gate, up):
-    return (gate * (1.0 / (1.0 + jnp.exp(-gate))) * up).astype(jnp.bfloat16)
+    half = 0.5 * gate
+    return ((half + half * jnp.tanh(half)) * up).astype(jnp.bfloat16)
 
 
 def dot_kernel(flip, counts, splits, term_counts, finished, narrow, ids, *refs):
@@ -341,7 +342,7 @@
     mx_count, first, ids, rows, tenants, sums_ref, far_ref, pick, scale, earlier_ref, out_ref, table, sums, far, held,
     tile_sem, held_sem,
 ):
-    block = pl.program_id(0)
+    turn = pl.program_id(0)
     tiles = far.shape[1] // BLOCK_ROWS
 
     def tile_copies(tile):
@@ -351,7 +352,7 @@
             for i, (source, target) in enumerate([(sums_ref, sums), (far_ref, far)])
         ]
 
-    @pl.when(block == 0)
+    @pl.when(turn == 0)
     def _():
         for tile in range(tiles):
             for copy in tile_copies(tile):
@@ -379,19 +380,22 @@
 
         held_copy.wait()
 
-    def find(slot, start):
-        return jnp.where(table[3, slot] == block, table[0, slot], start)
-
-    start = lax.fori_loop(0, len(SLOTS), find, jnp.int32(0))
-    count = rows[block]
-    base = pl.multiple_of(jnp.minimum(start // BLOCK_ROWS * BLOCK_ROWS, LIVE_ROWS - BLOCK_ROWS), BLOCK_ROWS)
-    shape = (BLOCK_ROWS, 2 * BLOCK_ROWS)
-    position = lax.broadcasted_iota(jnp.int32, shape, 0)
-    column = lax.broadcasted_iota(jnp.int32, shape, 1) + base
-    chosen = (position < count) & (column == position + start)
-    out_ref[...] = jnp.dot(
-        chosen.astype(jnp.bfloat16), held[pl.ds(base, 2 * BLOCK_ROWS), :], preferred_element_type=jnp.float32
-    ).astype(jnp.bfloat16)
+    for part in range(2):
+        block = 2 * turn + part
+
+        def find(slot, start, block=block):
+            return jnp.where(table[3, slot] == block, table[0, slot], start)
+
+        start = lax.fori_loop(0, len(SLOTS), find, jnp.int32(0))
+        count = rows[block]
+        base = pl.multiple_of(jnp.minimum(start // BLOCK_ROWS * BLOCK_ROWS, LIVE_ROWS - BLOCK_ROWS), BLOCK_ROWS)
+        shape = (BLOCK_ROWS, 2 * BLOCK_ROWS)
+        position = lax.broadcasted_iota(jnp.int32, shape, 0)
+        column = lax.broadcasted_iota(jnp.int32, shape, 1) + base
+        chosen = (position < count) & (column == position + start)
+        out_ref[part * BLOCK_ROWS:(part + 1) * BLOCK_ROWS, :] = jnp.dot(
+            chosen.astype(jnp.bfloat16), held[pl.ds(base, 2 * BLOCK_ROWS), :], preferred_element_type=jnp.float32
+        ).astype(jnp.bfloat16)
 
 
 def last_rows(mx_count, first, scalars, sums, far, pick, scale, earlier, blocks):
@@ -402,14 +406,14 @@
         out_shape=jax.ShapeDtypeStruct((blocks * BLOCK_ROWS, narrow), jnp.bfloat16),
         grid_spec=pltpu.PrefetchScalarGridSpec(
             num_scalar_prefetch=3,
-            grid=(blocks,),
+            grid=(blocks // 2,),
             in_specs=[
                 ANY, ANY,
                 pl.BlockSpec(pick.shape, lambda i, *_: (0, 0)),
                 pl.BlockSpec(scale.shape, lambda i, *_: (0, 0, 0)),
                 ANY,
             ],
-            out_specs=pl.BlockSpec((BLOCK_ROWS, narrow), lambda i, *_: (i, 0)),
+            out_specs=pl.BlockSpec((2 * BLOCK_ROWS, narrow), lambda i, *_: (i, 0)),
             scratch_shapes=[
                 pltpu.SMEM((4, len(SLOTS)), jnp.int32),
                 pltpu.VMEM(sums.shape, sums.dtype),

time: 192 us -> 192 us (level)
  no operation moved by 1% of the time
where the time goes in v1:
time: 192 us; the launch traced here: 190 us
  Pallas kernels  131 us (68%)
  waiting for transfers between devices  30.2 us (16%)
  starting transfers between devices  24.6 us (13%)
    pallas_call x9, Pallas kernels, dot_pair(): pl.pallas_call(functools.partial(dot_kernel, flip, counts, splits, term_c...  107 us
    ppermute x6, starting transfers between devices, hop(): return lax.ppermute(block, 'mx', pairs)  16.5 us
    pallas_call x3, Pallas kernels, pack_rows(): pl.pallas_call(functools.partial(pack_kernel, mx_count, first, rows_out,...  14.9 us
    ppermute x6, waiting for transfers between devices, hop(): return lax.ppermute(block, 'mx', pairs)  14.2 us
    ppermute x10, waiting for transfers between devices, swap(): return [lax.ppermute(part, 'my', pairs) for part in parts]  10.3 us
    pallas_call x1, Pallas kernels, last_rows(): pl.pallas_call(functools.partial(last_kernel, mx_count, first), out_shape...  9.86 us
  transfers between devices with their start and end apart: 21, of which 12 were waited for; matrix products, arithmetic and copies ran while one was open for 2% of the time, Pallas kernels for 61%

profile of v1, /device:TPU:8, one launch (start us, length us, event | category | flops | bytes accessed | tf_op | source)
XLA Modules:
  0.0 189.9 jit_solution(2199157514868302365)
XLA Ops:
  0.0 2.0 %collective-permute-start.1 = (bf16[256,2048]{1,0:T(8,128)(2,1)}, bf16[256,2048]{1,0:T(8,128)(2,1)}, u32[]{:S(2)}, u32[]{:S(2)}) collective-permute-start(bf16[256,2048]{1,0:T(8,128)(2,1)} %refs_0_.5), channel_id=1, source_target_pairs={{4,0},{8,4},{12,8},{5,1},{9,5},{13,9},{6,2},{10,6},{14,10},{7,3},{... | collective-permute-start | bytes 3145736 | tf_op jit(solution)/shard_map/ppermute | solution.py:453
  2.1 3.9 %collective-permute-start = (bf16[256,2048]{1,0:T(8,128)(2,1)}, bf16[256,2048]{1,0:T(8,128)(2,1)}, u32[]{:S(2)}, u32[]{:S(2)}) collective-permute-start(bf16[256,2048]{1,0:T(8,128)(2,1)} %refs_0_.5), channel_id=1, source_target_pairs={{0,4},{4,8},{8,12},{1,5},{5,9},{9,13},{2,6},{6,10},{10,14},{3,7},{... | collective-permute-start | bytes 3145736 | tf_op jit(solution)/shard_map/ppermute | solution.py:453
  10.9 2.9 %collective-permute-done.3 = f32[8,2,1664]{2,0,1:T(8,128)S(1)} collective-permute-done((f32[8,2,1664]{2,0,1:T(8,128)S(1)}, f32[8,2,1664]{2,0,1:T(8,128)S(1)}, u32[]{:S(2)}, u32[]{:S(2)}) %collective-permute-start.3) | collective-permute-done | bytes 106528 | tf_op jit(solution)/shard_map/ppermute | solution.py:461
  14.9 12.3 %collective-permute-done.1.refs_2_ = bf16[256,2048]{1,0:T(8,128)(2,1)} collective-permute-done((bf16[256,2048]{1,0:T(8,128)(2,1)}, bf16[256,2048]{1,0:T(8,128)(2,1)}, u32[]{:S(2)}, u32[]{:S(2)}) %collective-permute-start.1) | collective-permute-done | bytes 1048608 | tf_op jit(solution)/shard_map/ppermute | solution.py:453
  27.2 1.9 %collective-permute-done.refs_1_ = bf16[256,2048]{1,0:T(8,128)(2,1)} collective-permute-done((bf16[256,2048]{1,0:T(8,128)(2,1)}, bf16[256,2048]{1,0:T(8,128)(2,1)}, u32[]{:S(2)}, u32[]{:S(2)}) %collective-permute-start) | collective-permute-done | bytes 1048608 | tf_op jit(solution)/shard_map/ppermute | solution.py:453
  29.2 5.0 %pack_rows.3 = (bf16[256,2048]{1,0:T(8,128)(2,1)}, bf16[2,256,256]{2,1,0:T(8,128)(2,1)}, bf16[256,128]{1,0:T(8,128)(2,1)}, bf16[256,2048]{1,0:T(8,128)(2,1)}, bf16[256,2048]{1,0:T(8,128)(2,1)}) custom-call(s32[2]{0:T(128)} %pad_add_fusion.ids, s32[8]{0:T(128)} %rows.7, s32[8]{0:T(128)} %tenants.7, ...), custom_call_target="tpu_custom_call", output_to_operand_aliasing={{3}: (4, {}), {4}: (5, {})} | custom-call | tf_op jit(solution)/shard_map/pack_rows/pallas_call | solution.py:116
  34.2 4.7 %collective-permute-start.4 = (bf16[256,2048]{1,0:T(8,128)(2,1)}, bf16[256,2048]{1,0:T(8,128)(2,1)}, u32[]{:S(2)}, u32[]{:S(2)}) collective-permute-start(bf16[256,2048]{1,0:T(8,128)(2,1)} %get-tuple-element.29.refs_1_), channel_id=1, source_target_pairs={{4,8},{8,12},{5,9},{9,13},{6,10},{10,14},{7,11},{11,15},{20,24},{2... | collective-permute-start | bytes 3145736 | tf_op jit(solution)/shard_map/ppermute | solution.py:453
  38.9 1.9 %collective-permute-start.5 = (bf16[256,2048]{1,0:T(8,128)(2,1)}, bf16[256,2048]{1,0:T(8,128)(2,1)}, u32[]{:S(2)}, u32[]{:S(2)}) collective-permute-start(bf16[256,2048]{1,0:T(8,128)(2,1)} %get-tuple-element.30.refs_2_), channel_id=1, source_target_pairs={{4,0},{8,4},{5,1},{9,5},{6,2},{10,6},{7,3},{11,7},{20,16},{24,20},... | collective-permute-start | bytes 3145736 | tf_op jit(solution)/shard_map/ppermute | solution.py:453
  40.8 9.8 %dot_pair.8 = (bf16[256,1664]{1,0:T(8,128)(2,1)}, bf16[256,1664]{1,0:T(8,128)(2,1)}) custom-call(s32[2]{0:T(128)} %pad_add_fusion.ids, bf16[256,2048]{1,0:T(8,128)(2,1)} %get-tuple-element.28.refs_0_, bf16[2,256,256]{2,1,0:T(8,128)(2,1)} %get-tuple-element.31.refs_1_.refs_2_.refs_3_, bf16[2048,6656]{1,0:T(8,128)(2,1)} %refs_6_.3, ...), custom_call_target="tpu_custom_call" | custom-call | tf_op jit(solution)/shard_map/dot_pair/pallas_call | solution.py:309
  51.2 2.2 %collective-permute-done.6.refs_5_ = bf16[256,1664]{1,0:T(8,128)(2,1)} collective-permute-done((bf16[256,1664]{1,0:T(8,128)(2,1)}, bf16[256,1664]{1,0:T(8,128)(2,1)}, u32[]{:S(2)}, u32[]{:S(2)}) %collective-permute-start.6) | collective-permute-done | bytes 852000 | tf_op jit(solution)/shard_map/ppermute | solution.py:478
  54.6 9.9 %dot_pair.9.refs_6_ = bf16[2,256,1664]{2,1,0:T(8,128)(2,1)} custom-call(s32[2]{0:T(128)} %pad_add_fusion.ids, bf16[256,2048]{1,0:T(8,128)(2,1)} %get-tuple-element.28.refs_0_, bf16[2,256,256]{2,1,0:T(8,128)(2,1)} %get-tuple-element.31.refs_1_.refs_2_.refs_3_, bf16[2048,6656]{1,0:T(8,128)(2,1)} %refs_6_.3, bf16[2048,6656]{1,0:T(8,128)(2,1)} %refs_7_.1, ...), custom_call_target="tpu_custom_call" | custom-call | tf_op jit(solution)/shard_map/dot_pair/pallas_call | solution.py:309
  67.8 2.2 %collective-permute-start.9 = (bf16[256,2048]{1,0:T(8,128)(2,1)}, bf16[256,2048]{1,0:T(8,128)(2,1)}, u32[]{:S(2)}, u32[]{:S(2)}) collective-permute-start(bf16[256,2048]{1,0:T(8,128)(2,1)} %collective-permute-done.5.refs_4_), channel_id=1, source_target_pairs={{4,0},{5,1},{6,2},{7,3},{20,16},{21,17},{22,18},{23,19}} | collective-permute-start | bytes 3145736 | tf_op jit(solution)/shard_map/ppermute | solution.py:453
  70.1 5.1 %pack_rows.4 = (bf16[256,2048]{1,0:T(8,128)(2,1)}, bf16[2,256,256]{2,1,0:T(8,128)(2,1)}, bf16[256,128]{1,0:T(8,128)(2,1)}) custom-call(s32[2]{0:T(128)} %pad_add_fusion.ids, s32[8]{0:T(128)} %rows.7, s32[8]{0:T(128)} %tenants.7, bf16[256,2048]{1,0:T(8,128)(2,1)} %refs_0_.5, bf16[256,2048]{1,0:T(8,128)(2,1)} %get-tuple-element.29.refs_1_, ...), custom_call_target="tpu_custom_call" | custom-call | flops 999999995904 | tf_op jit(solution)/shard_map/pack_rows/pallas_call | solution.py:116
  75.1 9.8 %dot_pair.10 = (bf16[256,1664]{1,0:T(8,128)(2,1)}, bf16[256,1664]{1,0:T(8,128)(2,1)}) custom-call(s32[2]{0:T(128)} %pad_add_fusion.ids, bf16[256,2048]{1,0:T(8,128)(2,1)} %get-tuple-element.34.refs_0_.refs_1_, bf16[2,256,256]{2,1,0:T(8,128)(2,1)} %get-tuple-element.35.refs_1_.refs_3_.refs_4_, bf16[2048,6656]{1,0:T(8,128)(2,1)} %refs_6_.3, ...), custom_call_target="tpu_custom_call" | custom-call | tf_op jit(solution)/shard_map/dot_pair/pallas_call | solution.py:309
  85.5 2.2 %collective-permute-done.10.refs_5_ = bf16[256,1664]{1,0:T(8,128)(2,1)} collective-permute-done((bf16[256,1664]{1,0:T(8,128)(2,1)}, bf16[256,1664]{1,0:T(8,128)(2,1)}, u32[]{:S(2)}, u32[]{:S(2)}) %collective-permute-start.10) | collective-permute-done | bytes 852000 | tf_op jit(solution)/shard_map/ppermute | solution.py:478
  89.0 9.9 %dot_pair.11.refs_8_ = bf16[2,256,1664]{2,1,0:T(8,128)(2,1)} custom-call(s32[2]{0:T(128)} %pad_add_fusion.ids, bf16[256,2048]{1,0:T(8,128)(2,1)} %get-tuple-element.34.refs_0_.refs_1_, bf16[2,256,256]{2,1,0:T(8,128)(2,1)} %get-tuple-element.35.refs_1_.refs_3_.refs_4_, bf16[2048,6656]{1,0:T(8,128)(2,1)} %refs_6_.3, bf16[2048,6656]{1,0:T(8,128)(2,1)} %refs_7_.1, ...), custom_call_target="tpu_custom_call" | custom-call | tf_op jit(solution)/shard_map/dot_pair/pallas_call | solution.py:309
  99.5 4.8 %pack_rows.5 = (bf16[256,2048]{1,0:T(8,128)(2,1)}, bf16[2,256,256]{2,1,0:T(8,128)(2,1)}, bf16[256,128]{1,0:T(8,128)(2,1)}) custom-call(s32[2]{0:T(128)} %pad_add_fusion.ids, s32[8]{0:T(128)} %rows.7, s32[8]{0:T(128)} %tenants.7, bf16[256,2048]{1,0:T(8,128)(2,1)} %refs_0_.5, bf16[256,2048]{1,0:T(8,128)(2,1)} %get-tuple-element.29.refs_1_, ...), custom_call_target="tpu_custom_call" | custom-call | tf_op jit(solution)/shard_map/pack_rows/pallas_call | solution.py:116
  105.0 9.8 %dot_pair.12 = (bf16[256,1664]{1,0:T(8,128)(2,1)}, bf16[256,1664]{1,0:T(8,128)(2,1)}) custom-call(s32[2]{0:T(128)} %pad_add_fusion.ids, bf16[256,2048]{1,0:T(8,128)(2,1)} %get-tuple-element.38.refs_0_.refs_2_, bf16[2,256,256]{2,1,0:T(8,128)(2,1)} %get-tuple-element.39.refs_1_.refs_5_, bf16[2048,6656]{1,0:T(8,128)(2,1)} %refs_6_.3, ...), custom_call_target="tpu_custom_call" | custom-call | tf_op jit(solution)/shard_map/dot_pair/pallas_call | solution.py:309
  115.4 14.4 %dot_pair.13 = (bf16[512,1664]{1,0:T(8,128)(2,1)}, bf16[512,1664]{1,0:T(8,128)(2,1)}) custom-call(s32[2]{0:T(128)} %pad_add_fusion.ids, bf16[256,2048]{1,0:T(8,128)(2,1)} %get-tuple-element.28.refs_0_, bf16[256,2048]{1,0:T(8,128)(2,1)} %get-tuple-element.34.refs_0_.refs_1_, bf16[2,256,256]{2,1,0:T(8,128)(2,1)} %get-tuple-element.31.refs_1_.refs_2_.refs_3_, ...), custom_call_target="tpu_custom_call" | custom-call | tf_op jit(solution)/shard_map/dot_pair/pallas_call | solution.py:309
  130.3 9.9 %dot_pair.14.refs_5_ = bf16[2,256,1664]{2,1,0:T(8,128)(2,1)} custom-call(s32[2]{0:T(128)} %pad_add_fusion.ids, bf16[256,2048]{1,0:T(8,128)(2,1)} %get-tuple-element.38.refs_0_.refs_2_, bf16[2,256,256]{2,1,0:T(8,128)(2,1)} %get-tuple-element.39.refs_1_.refs_5_, bf16[2048,6656]{1,0:T(8,128)(2,1)} %refs_6_.3, bf16[2048,6656]{1,0:T(8,128)(2,1)} %refs_7_.1, ...), custom_call_target="tpu_custom_call" | custom-call | tf_op jit(solution)/shard_map/dot_pair/pallas_call | solution.py:309
  141.8 10.1 %dot_pair.15 = (bf16[256,1664]{1,0:T(8,128)(2,1)}, bf16[256,1664]{1,0:T(8,128)(2,1)}) custom-call(s32[2]{0:T(128)} %pad_add_fusion.ids, bf16[256,2048]{1,0:T(8,128)(2,1)} %get-tuple-element.38.refs_0_.refs_2_, bf16[2,256,256]{2,1,0:T(8,128)(2,1)} %get-tuple-element.39.refs_1_.refs_5_, bf16[2048,6656]{1,0:T(8,128)(2,1)} %refs_6_.3, ...), custom_call_target="tpu_custom_call" | custom-call | tf_op jit(solution)/shard_map/dot_pair/pallas_call | solution.py:309
  152.4 2.2 %collective-permute-done.17.refs_11_ = bf16[256,1664]{1,0:T(8,128)(2,1)} collective-permute-done((bf16[256,1664]{1,0:T(8,128)(2,1)}, bf16[256,1664]{1,0:T(8,128)(2,1)}, u32[]{:S(2)}, u32[]{:S(2)}) %collective-permute-start.17) | collective-permute-done | bytes 852000 | tf_op jit(solution)/shard_map/ppermute | solution.py:478
  155.9 23.1 %finish_dots.1 = (bf16[512,1664]{1,0:T(8,128)(2,1)}, f32[2,256,1664]{2,1,0:T(8,128)}) custom-call(s32[2]{0:T(128)} %pad_add_fusion.ids, bf16[256,2048]{1,0:T(8,128)(2,1)} %get-tuple-element.28.refs_0_, bf16[256,2048]{1,0:T(8,128)(2,1)} %get-tuple-element.34.refs_0_.refs_1_, bf16[256,2048]{1,0:T(8,128)(2,1)} %get-tuple-element.38.refs_0_.refs_2_, ...), custom_call_target="tpu_custom_call" | custom-call | tf_op jit(solution)/shard_map/finish_dots/pallas_call | solution.py:309
  179.8 9.9 %last_rows.1 = bf16[1024,1664]{1,0:T(8,128)(2,1)} custom-call(s32[2]{0:T(128)} %pad_add_fusion.ids, s32[8]{0:T(128)} %rows.7, s32[8]{0:T(128)} %tenants.7, f32[2,256,1664]{2,1,0:T(8,128)} %get-tuple-element.48.sums_ref, bf16[2,256,1664]{2,1,0:T(8,128)(2,1)} %collective-permute-done.20.far_ref, bf16[256,128]{1,0:T(8,128)(2,1)} %get-tuple-element.49.pick, ...), custom_call_target="tpu_custom_call" | custom-call | tf_op jit(solution)/shard_map/last_rows/pallas_call | solution.py:404
  (50 shorter events, 19.4 us)
Async XLA Ops:
  0.0 7.4 %copy-start = (f32[8,2,6656]{2,1,0:T(2,128)S(1)}, f32[8,2,6656]{2,1,0:T(2,128)}, u32[]{:S(2)}) copy-start(f32[8,2,6656]{2,1,0:T(2,128)} %param.14) | copy-start | bytes 1277956
  0.0 27.2 %collective-permute-start.1 = (bf16[256,2048]{1,0:T(8,128)(2,1)}, bf16[256,2048]{1,0:T(8,128)(2,1)}, u32[]{:S(2)}, u32[]{:S(2)}) collective-permute-start(bf16[256,2048]{1,0:T(8,128)(2,1)} %refs_0_.5), channel_id=1, source_target_pairs={{4,0},{8,4},{12,8},{5,1},{9,5},{13,9},{6,2},{10,6},{14,10},{7,3},{... | collective-permute-start | bytes 3145736 | tf_op jit(solution)/shard_map/ppermute | solution.py:453
  2.1 27.1 %collective-permute-start = (bf16[256,2048]{1,0:T(8,128)(2,1)}, bf16[256,2048]{1,0:T(8,128)(2,1)}, u32[]{:S(2)}, u32[]{:S(2)}) collective-permute-start(bf16[256,2048]{1,0:T(8,128)(2,1)} %refs_0_.5), channel_id=1, source_target_pairs={{0,4},{4,8},{8,12},{1,5},{5,9},{9,13},{2,6},{6,10},{10,14},{3,7},{... | collective-permute-start | bytes 3145736 | tf_op jit(solution)/shard_map/ppermute | solution.py:453
  7.2 1.5 collective-permute-start.2
  8.8 5.1 %collective-permute-start.3 = (f32[8,2,1664]{2,0,1:T(8,128)S(1)}, f32[8,2,1664]{2,0,1:T(8,128)S(1)}, u32[]{:S(2)}, u32[]{:S(2)}) collective-permute-start(f32[8,2,1664]{2,0,1:T(8,128)S(1)} %slice_bitcast_fusion), channel_id=1, source_target_pairs={{0,2},{1,3},{2,0},{3,1},{4,6},{5,7},{6,4},{7,5},{8,10},{9,11},{10,... | collective-permute-start | bytes 319496 | tf_op jit(solution)/shard_map/ppermute | solution.py:461
  34.2 31.9 %collective-permute-start.4 = (bf16[256,2048]{1,0:T(8,128)(2,1)}, bf16[256,2048]{1,0:T(8,128)(2,1)}, u32[]{:S(2)}, u32[]{:S(2)}) collective-permute-start(bf16[256,2048]{1,0:T(8,128)(2,1)} %get-tuple-element.29.refs_1_), channel_id=1, source_target_pairs={{4,8},{8,12},{5,9},{9,13},{6,10},{10,14},{7,11},{11,15},{20,24},{2... | collective-permute-start | bytes 3145736 | tf_op jit(solution)/shard_map/ppermute | solution.py:453
  38.9 28.9 %collective-permute-start.5 = (bf16[256,2048]{1,0:T(8,128)(2,1)}, bf16[256,2048]{1,0:T(8,128)(2,1)}, u32[]{:S(2)}, u32[]{:S(2)}) collective-permute-start(bf16[256,2048]{1,0:T(8,128)(2,1)} %get-tuple-element.30.refs_2_), channel_id=1, source_target_pairs={{4,0},{8,4},{5,1},{9,5},{6,2},{10,6},{7,3},{11,7},{20,16},{24,20},... | collective-permute-start | bytes 3145736 | tf_op jit(solution)/shard_map/ppermute | solution.py:453
  50.6 2.8 %collective-permute-start.6 = (bf16[256,1664]{1,0:T(8,128)(2,1)}, bf16[256,1664]{1,0:T(8,128)(2,1)}, u32[]{:S(2)}, u32[]{:S(2)}) collective-permute-start(bf16[256,1664]{1,0:T(8,128)(2,1)} %get-tuple-element.32), channel_id=1, source_target_pairs={{0,1},{1,0},{2,3},{3,2},{4,5},{5,4},{6,7},{7,6},{8,9},{9,8},{10,11... | collective-permute-start | bytes 2555912 | tf_op jit(solution)/shard_map/ppermute | solution.py:478
  50.7 3.9 %collective-permute-start.7 = (bf16[256,1664]{1,0:T(8,128)(2,1)}, bf16[256,1664]{1,0:T(8,128)(2,1)}, u32[]{:S(2)}, u32[]{:S(2)}) collective-permute-start(bf16[256,1664]{1,0:T(8,128)(2,1)} %get-tuple-element.33), channel_id=1, source_target_pairs={{0,1},{1,0},{2,3},{3,2},{4,5},{5,4},{6,7},{7,6},{8,9},{9,8},{10,11... | collective-permute-start | bytes 2555912 | tf_op jit(solution)/shard_map/ppermute | solution.py:478
  64.6 40.4 %collective-permute-start.12 = (bf16[2,256,1664]{2,1,0:T(8,128)(2,1)}, bf16[2,256,1664]{2,1,0:T(8,128)(2,1)}, u32[]{:S(2)}, u32[]{:S(2)}) collective-permute-start(bf16[2,256,1664]{2,1,0:T(8,128)(2,1)} %dot_pair.9.refs_6_), channel_id=1, source_target_pairs={{0,2},{1,3},{2,0},{3,1},{4,6},{5,7},{6,4},{7,5},{8,10},{9,11},{10,... | collective-permute-start | bytes 5111816 | tf_op jit(solution)/shard_map/ppermute | solution.py:485
  66.1 33.4 %collective-permute-start.8 = (bf16[256,2048]{1,0:T(8,128)(2,1)}, bf16[256,2048]{1,0:T(8,128)(2,1)}, u32[]{:S(2)}, u32[]{:S(2)}) collective-permute-start(bf16[256,2048]{1,0:T(8,128)(2,1)} %collective-permute-done.4.refs_3_), channel_id=1, source_target_pairs={{8,12},{9,13},{10,14},{11,15},{24,28},{25,29},{26,30},{27,31}} | collective-permute-start | bytes 3145736 | tf_op jit(solution)/shard_map/ppermute | solution.py:453
  67.8 31.7 %collective-permute-start.9 = (bf16[256,2048]{1,0:T(8,128)(2,1)}, bf16[256,2048]{1,0:T(8,128)(2,1)}, u32[]{:S(2)}, u32[]{:S(2)}) collective-permute-start(bf16[256,2048]{1,0:T(8,128)(2,1)} %collective-permute-done.5.refs_4_), channel_id=1, source_target_pairs={{4,0},{5,1},{6,2},{7,3},{20,16},{21,17},{22,18},{23,19}} | collective-permute-start | bytes 3145736 | tf_op jit(solution)/shard_map/ppermute | solution.py:453
  85.0 2.8 %collective-permute-start.10 = (bf16[256,1664]{1,0:T(8,128)(2,1)}, bf16[256,1664]{1,0:T(8,128)(2,1)}, u32[]{:S(2)}, u32[]{:S(2)}) collective-permute-start(bf16[256,1664]{1,0:T(8,128)(2,1)} %get-tuple-element.36), channel_id=1, source_target_pairs={{0,1},{1,0},{2,3},{3,2},{4,5},{5,4},{6,7},{7,6},{8,9},{9,8},{10,11... | collective-permute-start | bytes 2555912 | tf_op jit(solution)/shard_map/ppermute | solution.py:478
  85.1 3.9 %collective-permute-start.11 = (bf16[256,1664]{1,0:T(8,128)(2,1)}, bf16[256,1664]{1,0:T(8,128)(2,1)}, u32[]{:S(2)}, u32[]{:S(2)}) collective-permute-start(bf16[256,1664]{1,0:T(8,128)(2,1)} %get-tuple-element.37), channel_id=1, source_target_pairs={{0,1},{1,0},{2,3},{3,2},{4,5},{5,4},{6,7},{7,6},{8,9},{9,8},{10,11... | collective-permute-start | bytes 2555912 | tf_op jit(solution)/shard_map/ppermute | solution.py:478
  98.9 53.0 %collective-permute-start.19 = (bf16[2,256,1664]{2,1,0:T(8,128)(2,1)}, bf16[2,256,1664]{2,1,0:T(8,128)(2,1)}, u32[]{:S(2)}, u32[]{:S(2)}) collective-permute-start(bf16[2,256,1664]{2,1,0:T(8,128)(2,1)} %dot_pair.11.refs_8_), channel_id=1, source_target_pairs={{0,2},{1,3},{2,0},{3,1},{4,6},{5,7},{6,4},{7,5},{8,10},{9,11},{10,... | collective-permute-start | bytes 5111816 | tf_op jit(solution)/shard_map/ppermute | solution.py:485
  114.8 15.5 %collective-permute-start.16 = (bf16[256,1664]{1,0:T(8,128)(2,1)}, bf16[256,1664]{1,0:T(8,128)(2,1)}, u32[]{:S(2)}, u32[]{:S(2)}) collective-permute-start(bf16[256,1664]{1,0:T(8,128)(2,1)} %get-tuple-element.43), channel_id=1, source_target_pairs={{0,1},{1,0},{2,3},{3,2},{4,5},{5,4},{6,7},{7,6},{8,9},{9,8},{10,11... | collective-permute-start | bytes 2555912 | tf_op jit(solution)/shard_map/ppermute | solution.py:478
  114.9 15.4 %collective-permute-start.15 = (bf16[256,1664]{1,0:T(8,128)(2,1)}, bf16[256,1664]{1,0:T(8,128)(2,1)}, u32[]{:S(2)}, u32[]{:S(2)}) collective-permute-start(bf16[256,1664]{1,0:T(8,128)(2,1)} %get-tuple-element.40.refs_7_), channel_id=1, source_target_pairs={{0,1},{1,0},{2,3},{3,2},{4,5},{5,4},{6,7},{7,6},{8,9},{9,8},{10,11... | collective-permute-start | bytes 2555912 | tf_op jit(solution)/shard_map/ppermute | solution.py:478
  129.8 26.1 %collective-permute-start.14 = (bf16[512,1664]{1,0:T(8,128)(2,1)}, bf16[512,1664]{1,0:T(8,128)(2,1)}, u32[]{:S(2)}, u32[]{:S(2)}) collective-permute-start(bf16[512,1664]{1,0:T(8,128)(2,1)} %get-tuple-element.42), channel_id=1, source_target_pairs={{0,1},{1,0},{2,3},{3,2},{4,5},{5,4},{6,7},{7,6},{8,9},{9,8},{10,11... | collective-permute-start | bytes 5111816 | tf_op jit(solution)/shard_map/ppermute | solution.py:478
  129.9 25.9 %collective-permute-start.13 = (bf16[512,1664]{1,0:T(8,128)(2,1)}, bf16[512,1664]{1,0:T(8,128)(2,1)}, u32[]{:S(2)}, u32[]{:S(2)}) collective-permute-start(bf16[512,1664]{1,0:T(8,128)(2,1)} %get-tuple-element.41.refs_7_), channel_id=1, source_target_pairs={{0,1},{1,0},{2,3},{3,2},{4,5},{5,4},{6,7},{7,6},{8,9},{9,8},{10,11... | collective-permute-start | bytes 5111816 | tf_op jit(solution)/shard_map/ppermute | solution.py:478
  140.3 39.5 %collective-permute-start.20 = (bf16[2,256,1664]{2,1,0:T(8,128)(2,1)}, bf16[2,256,1664]{2,1,0:T(8,128)(2,1)}, u32[]{:S(2)}, u32[]{:S(2)}) collective-permute-start(bf16[2,256,1664]{2,1,0:T(8,128)(2,1)} %dot_pair.14.refs_5_), channel_id=1, source_target_pairs={{0,2},{1,3},{2,0},{3,1},{4,6},{5,7},{6,4},{7,5},{8,10},{9,11},{10,... | collective-permute-start | bytes 5111816 | tf_op jit(solution)/shard_map/ppermute | solution.py:485
  151.8 2.8 %collective-permute-start.17 = (bf16[256,1664]{1,0:T(8,128)(2,1)}, bf16[256,1664]{1,0:T(8,128)(2,1)}, u32[]{:S(2)}, u32[]{:S(2)}) collective-permute-start(bf16[256,1664]{1,0:T(8,128)(2,1)} %get-tuple-element.44), channel_id=1, source_target_pairs={{0,1},{1,0},{2,3},{3,2},{4,5},{5,4},{6,7},{7,6},{8,9},{9,8},{10,11... | collective-permute-start | bytes 2555912 | tf_op jit(solution)/shard_map/ppermute | solution.py:478
  151.9 3.9 %collective-permute-start.18 = (bf16[256,1664]{1,0:T(8,128)(2,1)}, bf16[256,1664]{1,0:T(8,128)(2,1)}, u32[]{:S(2)}, u32[]{:S(2)}) collective-permute-start(bf16[256,1664]{1,0:T(8,128)(2,1)} %get-tuple-element.45), channel_id=1, source_target_pairs={{0,1},{1,0},{2,3},{3,2},{4,5},{5,4},{6,7},{7,6},{8,9},{9,8},{10,11... | collective-permute-start | bytes 2555912 | tf_op jit(solution)/shard_map/ppermute | solution.py:478
  179.8 9.9 %copy-start.1 = (f32[8,2,6656]{2,1,0:T(2,128)S(1)}, f32[8,2,6656]{2,1,0:T(2,128)}, u32[]{:S(2)}) copy-start(f32[8,2,6656]{2,1,0:T(2,128)} %param.14) | copy-start | bytes 1277956

commit v2 on v1

--- a/solution.py
+++ b/solution.py
@@ -240,8 +240,7 @@
 
         depths = pl.ds(pl.multiple_of(step * STEP_DEPTH, STEP_DEPTH), STEP_DEPTH)
 
-        @pl.loop(0, 2)
-        def _(side):
+        for side in range(2):
             acc[side] += jnp.dot(x[:, depths], w[side, step], preferred_element_type=jnp.float32)
 
     for copy in loads[first_loads:]:

time: 192 us -> 190 us (0.990)
  Pallas kernels: 131 us -> 128 us
    pallas_call x9, Pallas kernels: 107 us -> 103 us  [dot_pair(): pl.pallas_call(functools.partial(dot_kernel, flip, counts, splits, term_c...]
  transfers between devices with their start and end apart: 21 -> 21, of which waited for: 12 -> 12; matrix products, arithmetic and copies ran while one was open for 2% -> 2% of each run, Pallas kernels for 61% -> 60%
where the time goes in v2:
time: 190 us; the launch traced here: 188 us
  Pallas kernels  128 us (67%)
  waiting for transfers between devices  31.8 us (17%)
  starting transfers between devices  24.2 us (13%)
    pallas_call x9, Pallas kernels, dot_pair(): pl.pallas_call(functools.partial(dot_kernel, flip, counts, splits, term_c...  103 us
    ppermute x6, starting transfers between devices, hop(): return lax.ppermute(block, 'mx', pairs)  16.1 us
    pallas_call x3, Pallas kernels, pack_rows(): pl.pallas_call(functools.partial(pack_kernel, mx_count, first, rows_out,...  15.3 us
    ppermute x6, waiting for transfers between devices, hop(): return lax.ppermute(block, 'mx', pairs)  14.2 us
    ppermute x10, waiting for transfers between devices, swap(): return [lax.ppermute(part, 'my', pairs) for part in parts]  10.3 us
    pallas_call x1, Pallas kernels, last_rows(): pl.pallas_call(functools.partial(last_kernel, mx_count, first), out_shape...  9.87 us
  transfers between devices with their start and end apart: 21, of which 12 were waited for; matrix products, arithmetic and copies ran while one was open for 2% of the time, Pallas kernels for 60%

profile of v2, /device:TPU:8, one launch (start us, length us, event | category | flops | bytes accessed | tf_op | source)
XLA Modules:
  0.0 187.5 jit_solution(6713909851447421143)
XLA Ops:
  0.0 2.0 %collective-permute-start.1 = (bf16[256,2048]{1,0:T(8,128)(2,1)}, bf16[256,2048]{1,0:T(8,128)(2,1)}, u32[]{:S(2)}, u32[]{:S(2)}) collective-permute-start(bf16[256,2048]{1,0:T(8,128)(2,1)} %refs_0_.5), channel_id=1, source_target_pairs={{4,0},{8,4},{12,8},{5,1},{9,5},{13,9},{6,2},{10,6},{14,10},{7,3},{... | collective-permute-start | bytes 3145736 | tf_op jit(solution)/shard_map/ppermute | solution.py:452
  2.1 3.9 %collective-permute-start = (bf16[256,2048]{1,0:T(8,128)(2,1)}, bf16[256,2048]{1,0:T(8,128)(2,1)}, u32[]{:S(2)}, u32[]{:S(2)}) collective-permute-start(bf16[256,2048]{1,0:T(8,128)(2,1)} %refs_0_.5), channel_id=1, source_target_pairs={{0,4},{4,8},{8,12},{1,5},{5,9},{9,13},{2,6},{6,10},{10,14},{3,7},{... | collective-permute-start | bytes 3145736 | tf_op jit(solution)/shard_map/ppermute | solution.py:452
  10.9 2.9 %collective-permute-done.3 = f32[8,2,1664]{2,0,1:T(8,128)S(1)} collective-permute-done((f32[8,2,1664]{2,0,1:T(8,128)S(1)}, f32[8,2,1664]{2,0,1:T(8,128)S(1)}, u32[]{:S(2)}, u32[]{:S(2)}) %collective-permute-start.3) | collective-permute-done | bytes 106528 | tf_op jit(solution)/shard_map/ppermute | solution.py:460
  14.9 12.3 %collective-permute-done.1.refs_2_ = bf16[256,2048]{1,0:T(8,128)(2,1)} collective-permute-done((bf16[256,2048]{1,0:T(8,128)(2,1)}, bf16[256,2048]{1,0:T(8,128)(2,1)}, u32[]{:S(2)}, u32[]{:S(2)}) %collective-permute-start.1) | collective-permute-done | bytes 1048608 | tf_op jit(solution)/shard_map/ppermute | solution.py:452
  27.2 1.9 %collective-permute-done.refs_1_ = bf16[256,2048]{1,0:T(8,128)(2,1)} collective-permute-done((bf16[256,2048]{1,0:T(8,128)(2,1)}, bf16[256,2048]{1,0:T(8,128)(2,1)}, u32[]{:S(2)}, u32[]{:S(2)}) %collective-permute-start) | collective-permute-done | bytes 1048608 | tf_op jit(solution)/shard_map/ppermute | solution.py:452
  29.2 5.0 %pack_rows.3 = (bf16[256,2048]{1,0:T(8,128)(2,1)}, bf16[2,256,256]{2,1,0:T(8,128)(2,1)}, bf16[256,128]{1,0:T(8,128)(2,1)}, bf16[256,2048]{1,0:T(8,128)(2,1)}, bf16[256,2048]{1,0:T(8,128)(2,1)}) custom-call(s32[2]{0:T(128)} %pad_add_fusion.ids, s32[8]{0:T(128)} %rows.7, s32[8]{0:T(128)} %tenants.7, ...), custom_call_target="tpu_custom_call", output_to_operand_aliasing={{3}: (4, {}), {4}: (5, {})} | custom-call | tf_op jit(solution)/shard_map/pack_rows/pallas_call | solution.py:116
  34.2 4.3 %collective-permute-start.4 = (bf16[256,2048]{1,0:T(8,128)(2,1)}, bf16[256,2048]{1,0:T(8,128)(2,1)}, u32[]{:S(2)}, u32[]{:S(2)}) collective-permute-start(bf16[256,2048]{1,0:T(8,128)(2,1)} %get-tuple-element.29.refs_1_), channel_id=1, source_target_pairs={{4,8},{8,12},{5,9},{9,13},{6,10},{10,14},{7,11},{11,15},{20,24},{2... | collective-permute-start | bytes 3145736 | tf_op jit(solution)/shard_map/ppermute | solution.py:452
  40.4 9.3 %dot_pair.8 = (bf16[256,1664]{1,0:T(8,128)(2,1)}, bf16[256,1664]{1,0:T(8,128)(2,1)}) custom-call(s32[2]{0:T(128)} %pad_add_fusion.ids, bf16[256,2048]{1,0:T(8,128)(2,1)} %get-tuple-element.28.refs_0_, bf16[2,256,256]{2,1,0:T(8,128)(2,1)} %get-tuple-element.31.refs_1_.refs_2_.refs_3_, bf16[2048,6656]{1,0:T(8,128)(2,1)} %refs_6_.3, ...), custom_call_target="tpu_custom_call" | custom-call | tf_op jit(solution)/shard_map/dot_pair/pallas_call | solution.py:308
  50.3 2.2 %collective-permute-done.6.refs_5_ = bf16[256,1664]{1,0:T(8,128)(2,1)} collective-permute-done((bf16[256,1664]{1,0:T(8,128)(2,1)}, bf16[256,1664]{1,0:T(8,128)(2,1)}, u32[]{:S(2)}, u32[]{:S(2)}) %collective-permute-start.6) | collective-permute-done | bytes 852000 | tf_op jit(solution)/shard_map/ppermute | solution.py:477
  53.7 9.7 %dot_pair.9.refs_6_ = bf16[2,256,1664]{2,1,0:T(8,128)(2,1)} custom-call(s32[2]{0:T(128)} %pad_add_fusion.ids, bf16[256,2048]{1,0:T(8,128)(2,1)} %get-tuple-element.28.refs_0_, bf16[2,256,256]{2,1,0:T(8,128)(2,1)} %get-tuple-element.31.refs_1_.refs_2_.refs_3_, bf16[2048,6656]{1,0:T(8,128)(2,1)} %refs_6_.3, bf16[2048,6656]{1,0:T(8,128)(2,1)} %refs_7_.1, ...), custom_call_target="tpu_custom_call" | custom-call | tf_op jit(solution)/shard_map/dot_pair/pallas_call | solution.py:308
  66.7 2.2 %collective-permute-start.9 = (bf16[256,2048]{1,0:T(8,128)(2,1)}, bf16[256,2048]{1,0:T(8,128)(2,1)}, u32[]{:S(2)}, u32[]{:S(2)}) collective-permute-start(bf16[256,2048]{1,0:T(8,128)(2,1)} %collective-permute-done.5.refs_4_), channel_id=1, source_target_pairs={{4,0},{5,1},{6,2},{7,3},{20,16},{21,17},{22,18},{23,19}} | collective-permute-start | bytes 3145736 | tf_op jit(solution)/shard_map/ppermute | solution.py:452
  68.9 5.1 %pack_rows.4 = (bf16[256,2048]{1,0:T(8,128)(2,1)}, bf16[2,256,256]{2,1,0:T(8,128)(2,1)}, bf16[256,128]{1,0:T(8,128)(2,1)}) custom-call(s32[2]{0:T(128)} %pad_add_fusion.ids, s32[8]{0:T(128)} %rows.7, s32[8]{0:T(128)} %tenants.7, bf16[256,2048]{1,0:T(8,128)(2,1)} %refs_0_.5, bf16[256,2048]{1,0:T(8,128)(2,1)} %get-tuple-element.29.refs_1_, ...), custom_call_target="tpu_custom_call" | custom-call | flops 999999995904 | tf_op jit(solution)/shard_map/pack_rows/pallas_call | solution.py:116
  74.0 9.3 %dot_pair.10 = (bf16[256,1664]{1,0:T(8,128)(2,1)}, bf16[256,1664]{1,0:T(8,128)(2,1)}) custom-call(s32[2]{0:T(128)} %pad_add_fusion.ids, bf16[256,2048]{1,0:T(8,128)(2,1)} %get-tuple-element.34.refs_0_.refs_1_, bf16[2,256,256]{2,1,0:T(8,128)(2,1)} %get-tuple-element.35.refs_1_.refs_3_.refs_4_, bf16[2048,6656]{1,0:T(8,128)(2,1)} %refs_6_.3, ...), custom_call_target="tpu_custom_call" | custom-call | tf_op jit(solution)/shard_map/dot_pair/pallas_call | solution.py:308
  83.9 2.2 %collective-permute-done.10.refs_5_ = bf16[256,1664]{1,0:T(8,128)(2,1)} collective-permute-done((bf16[256,1664]{1,0:T(8,128)(2,1)}, bf16[256,1664]{1,0:T(8,128)(2,1)}, u32[]{:S(2)}, u32[]{:S(2)}) %collective-permute-start.10) | collective-permute-done | bytes 852000 | tf_op jit(solution)/shard_map/ppermute | solution.py:477
  87.3 9.7 %dot_pair.11.refs_8_ = bf16[2,256,1664]{2,1,0:T(8,128)(2,1)} custom-call(s32[2]{0:T(128)} %pad_add_fusion.ids, bf16[256,2048]{1,0:T(8,128)(2,1)} %get-tuple-element.34.refs_0_.refs_1_, bf16[2,256,256]{2,1,0:T(8,128)(2,1)} %get-tuple-element.35.refs_1_.refs_3_.refs_4_, bf16[2048,6656]{1,0:T(8,128)(2,1)} %refs_6_.3, bf16[2048,6656]{1,0:T(8,128)(2,1)} %refs_7_.1, ...), custom_call_target="tpu_custom_call" | custom-call | tf_op jit(solution)/shard_map/dot_pair/pallas_call | solution.py:308
  97.7 5.2 %pack_rows.5 = (bf16[256,2048]{1,0:T(8,128)(2,1)}, bf16[2,256,256]{2,1,0:T(8,128)(2,1)}, bf16[256,128]{1,0:T(8,128)(2,1)}) custom-call(s32[2]{0:T(128)} %pad_add_fusion.ids, s32[8]{0:T(128)} %rows.7, s32[8]{0:T(128)} %tenants.7, bf16[256,2048]{1,0:T(8,128)(2,1)} %refs_0_.5, bf16[256,2048]{1,0:T(8,128)(2,1)} %get-tuple-element.29.refs_1_, ...), custom_call_target="tpu_custom_call" | custom-call | tf_op jit(solution)/shard_map/pack_rows/pallas_call | solution.py:116
  103.9 9.3 %dot_pair.12 = (bf16[256,1664]{1,0:T(8,128)(2,1)}, bf16[256,1664]{1,0:T(8,128)(2,1)}) custom-call(s32[2]{0:T(128)} %pad_add_fusion.ids, bf16[256,2048]{1,0:T(8,128)(2,1)} %get-tuple-element.38.refs_0_.refs_2_, bf16[2,256,256]{2,1,0:T(8,128)(2,1)} %get-tuple-element.39.refs_1_.refs_5_, bf16[2048,6656]{1,0:T(8,128)(2,1)} %refs_6_.3, ...), custom_call_target="tpu_custom_call" | custom-call | tf_op jit(solution)/shard_map/dot_pair/pallas_call | solution.py:308
  113.7 13.8 %dot_pair.13 = (bf16[512,1664]{1,0:T(8,128)(2,1)}, bf16[512,1664]{1,0:T(8,128)(2,1)}) custom-call(s32[2]{0:T(128)} %pad_add_fusion.ids, bf16[256,2048]{1,0:T(8,128)(2,1)} %get-tuple-element.28.refs_0_, bf16[256,2048]{1,0:T(8,128)(2,1)} %get-tuple-element.34.refs_0_.refs_1_, bf16[2,256,256]{2,1,0:T(8,128)(2,1)} %get-tuple-element.31.refs_1_.refs_2_.refs_3_, ...), custom_call_target="tpu_custom_call" | custom-call | tf_op jit(solution)/shard_map/dot_pair/pallas_call | solution.py:308
  128.2 9.7 %dot_pair.14.refs_5_ = bf16[2,256,1664]{2,1,0:T(8,128)(2,1)} custom-call(s32[2]{0:T(128)} %pad_add_fusion.ids, bf16[256,2048]{1,0:T(8,128)(2,1)} %get-tuple-element.38.refs_0_.refs_2_, bf16[2,256,256]{2,1,0:T(8,128)(2,1)} %get-tuple-element.39.refs_1_.refs_5_, bf16[2048,6656]{1,0:T(8,128)(2,1)} %refs_6_.3, bf16[2048,6656]{1,0:T(8,128)(2,1)} %refs_7_.1, ...), custom_call_target="tpu_custom_call" | custom-call | tf_op jit(solution)/shard_map/dot_pair/pallas_call | solution.py:308
  139.4 9.3 %dot_pair.15 = (bf16[256,1664]{1,0:T(8,128)(2,1)}, bf16[256,1664]{1,0:T(8,128)(2,1)}) custom-call(s32[2]{0:T(128)} %pad_add_fusion.ids, bf16[256,2048]{1,0:T(8,128)(2,1)} %get-tuple-element.38.refs_0_.refs_2_, bf16[2,256,256]{2,1,0:T(8,128)(2,1)} %get-tuple-element.39.refs_1_.refs_5_, bf16[2048,6656]{1,0:T(8,128)(2,1)} %refs_6_.3, ...), custom_call_target="tpu_custom_call" | custom-call | tf_op jit(solution)/shard_map/dot_pair/pallas_call | solution.py:308
  149.3 2.2 %collective-permute-done.17.refs_11_ = bf16[256,1664]{1,0:T(8,128)(2,1)} collective-permute-done((bf16[256,1664]{1,0:T(8,128)(2,1)}, bf16[256,1664]{1,0:T(8,128)(2,1)}, u32[]{:S(2)}, u32[]{:S(2)}) %collective-permute-start.17) | collective-permute-done | bytes 852000 | tf_op jit(solution)/shard_map/ppermute | solution.py:477
  152.8 22.6 %finish_dots.1 = (bf16[512,1664]{1,0:T(8,128)(2,1)}, f32[2,256,1664]{2,1,0:T(8,128)}) custom-call(s32[2]{0:T(128)} %pad_add_fusion.ids, bf16[256,2048]{1,0:T(8,128)(2,1)} %get-tuple-element.28.refs_0_, bf16[256,2048]{1,0:T(8,128)(2,1)} %get-tuple-element.34.refs_0_.refs_1_, bf16[256,2048]{1,0:T(8,128)(2,1)} %get-tuple-element.38.refs_0_.refs_2_, ...), custom_call_target="tpu_custom_call" | custom-call | tf_op jit(solution)/shard_map/finish_dots/pallas_call | solution.py:308
  175.3 2.1 %collective-permute-done.20.far_ref = bf16[2,256,1664]{2,1,0:T(8,128)(2,1)} collective-permute-done((bf16[2,256,1664]{2,1,0:T(8,128)(2,1)}, bf16[2,256,1664]{2,1,0:T(8,128)(2,1)}, u32[]{:S(2)}, u32[]{:S(2)}) %collective-permute-start.20) | collective-permute-done | bytes 1703968 | tf_op jit(solution)/shard_map/ppermute | solution.py:484
  177.5 9.9 %last_rows.1 = bf16[1024,1664]{1,0:T(8,128)(2,1)} custom-call(s32[2]{0:T(128)} %pad_add_fusion.ids, s32[8]{0:T(128)} %rows.7, s32[8]{0:T(128)} %tenants.7, f32[2,256,1664]{2,1,0:T(8,128)} %get-tuple-element.48.sums_ref, bf16[2,256,1664]{2,1,0:T(8,128)(2,1)} %collective-permute-done.20.far_ref, bf16[256,128]{1,0:T(8,128)(2,1)} %get-tuple-element.49.pick, ...), custom_call_target="tpu_custom_call" | custom-call | tf_op jit(solution)/shard_map/last_rows/pallas_call | solution.py:403
  (50 shorter events, 20.7 us)
Async XLA Ops:
  0.0 7.4 %copy-start = (f32[8,2,6656]{2,1,0:T(2,128)S(1)}, f32[8,2,6656]{2,1,0:T(2,128)}, u32[]{:S(2)}) copy-start(f32[8,2,6656]{2,1,0:T(2,128)} %param.14) | copy-start | bytes 1277956
  0.0 27.2 %collective-permute-start.1 = (bf16[256,2048]{1,0:T(8,128)(2,1)}, bf16[256,2048]{1,0:T(8,128)(2,1)}, u32[]{:S(2)}, u32[]{:S(2)}) collective-permute-start(bf16[256,2048]{1,0:T(8,128)(2,1)} %refs_0_.5), channel_id=1, source_target_pairs={{4,0},{8,4},{12,8},{5,1},{9,5},{13,9},{6,2},{10,6},{14,10},{7,3},{... | collective-permute-start | bytes 3145736 | tf_op jit(solution)/shard_map/ppermute | solution.py:452
  2.1 27.1 %collective-permute-start = (bf16[256,2048]{1,0:T(8,128)(2,1)}, bf16[256,2048]{1,0:T(8,128)(2,1)}, u32[]{:S(2)}, u32[]{:S(2)}) collective-permute-start(bf16[256,2048]{1,0:T(8,128)(2,1)} %refs_0_.5), channel_id=1, source_target_pairs={{0,4},{4,8},{8,12},{1,5},{5,9},{9,13},{2,6},{6,10},{10,14},{3,7},{... | collective-permute-start | bytes 3145736 | tf_op jit(solution)/shard_map/ppermute | solution.py:452
  7.2 1.5 collective-permute-start.2
  8.8 5.1 %collective-permute-start.3 = (f32[8,2,1664]{2,0,1:T(8,128)S(1)}, f32[8,2,1664]{2,0,1:T(8,128)S(1)}, u32[]{:S(2)}, u32[]{:S(2)}) collective-permute-start(f32[8,2,1664]{2,0,1:T(8,128)S(1)} %slice_bitcast_fusion), channel_id=1, source_target_pairs={{0,2},{1,3},{2,0},{3,1},{4,6},{5,7},{6,4},{7,5},{8,10},{9,11},{10,... | collective-permute-start | bytes 319496 | tf_op jit(solution)/shard_map/ppermute | solution.py:460
  34.2 30.8 %collective-permute-start.4 = (bf16[256,2048]{1,0:T(8,128)(2,1)}, bf16[256,2048]{1,0:T(8,128)(2,1)}, u32[]{:S(2)}, u32[]{:S(2)}) collective-permute-start(bf16[256,2048]{1,0:T(8,128)(2,1)} %get-tuple-element.29.refs_1_), channel_id=1, source_target_pairs={{4,8},{8,12},{5,9},{9,13},{6,10},{10,14},{7,11},{11,15},{20,24},{2... | collective-permute-start | bytes 3145736 | tf_op jit(solution)/shard_map/ppermute | solution.py:452
  38.5 28.2 %collective-permute-start.5 = (bf16[256,2048]{1,0:T(8,128)(2,1)}, bf16[256,2048]{1,0:T(8,128)(2,1)}, u32[]{:S(2)}, u32[]{:S(2)}) collective-permute-start(bf16[256,2048]{1,0:T(8,128)(2,1)} %get-tuple-element.30.refs_2_), channel_id=1, source_target_pairs={{4,0},{8,4},{5,1},{9,5},{6,2},{10,6},{7,3},{11,7},{20,16},{24,20},... | collective-permute-start | bytes 3145736 | tf_op jit(solution)/shard_map/ppermute | solution.py:452
  49.7 2.8 %collective-permute-start.6 = (bf16[256,1664]{1,0:T(8,128)(2,1)}, bf16[256,1664]{1,0:T(8,128)(2,1)}, u32[]{:S(2)}, u32[]{:S(2)}) collective-permute-start(bf16[256,1664]{1,0:T(8,128)(2,1)} %get-tuple-element.32), channel_id=1, source_target_pairs={{0,1},{1,0},{2,3},{3,2},{4,5},{5,4},{6,7},{7,6},{8,9},{9,8},{10,11... | collective-permute-start | bytes 2555912 | tf_op jit(solution)/shard_map/ppermute | solution.py:477
  49.8 3.9 %collective-permute-start.7 = (bf16[256,1664]{1,0:T(8,128)(2,1)}, bf16[256,1664]{1,0:T(8,128)(2,1)}, u32[]{:S(2)}, u32[]{:S(2)}) collective-permute-start(bf16[256,1664]{1,0:T(8,128)(2,1)} %get-tuple-element.33), channel_id=1, source_target_pairs={{0,1},{1,0},{2,3},{3,2},{4,5},{5,4},{6,7},{7,6},{8,9},{9,8},{10,11... | collective-permute-start | bytes 2555912 | tf_op jit(solution)/shard_map/ppermute | solution.py:477
  63.4 40.4 %collective-permute-start.12 = (bf16[2,256,1664]{2,1,0:T(8,128)(2,1)}, bf16[2,256,1664]{2,1,0:T(8,128)(2,1)}, u32[]{:S(2)}, u32[]{:S(2)}) collective-permute-start(bf16[2,256,1664]{2,1,0:T(8,128)(2,1)} %dot_pair.9.refs_6_), channel_id=1, source_target_pairs={{0,2},{1,3},{2,0},{3,1},{4,6},{5,7},{6,4},{7,5},{8,10},{9,11},{10,... | collective-permute-start | bytes 5111816 | tf_op jit(solution)/shard_map/ppermute | solution.py:484
  65.0 32.8 %collective-permute-start.8 = (bf16[256,2048]{1,0:T(8,128)(2,1)}, bf16[256,2048]{1,0:T(8,128)(2,1)}, u32[]{:S(2)}, u32[]{:S(2)}) collective-permute-start(bf16[256,2048]{1,0:T(8,128)(2,1)} %collective-permute-done.4.refs_3_), channel_id=1, source_target_pairs={{8,12},{9,13},{10,14},{11,15},{24,28},{25,29},{26,30},{27,31}} | collective-permute-start | bytes 3145736 | tf_op jit(solution)/shard_map/ppermute | solution.py:452
  66.7 31.0 %collective-permute-start.9 = (bf16[256,2048]{1,0:T(8,128)(2,1)}, bf16[256,2048]{1,0:T(8,128)(2,1)}, u32[]{:S(2)}, u32[]{:S(2)}) collective-permute-start(bf16[256,2048]{1,0:T(8,128)(2,1)} %collective-permute-done.5.refs_4_), channel_id=1, source_target_pairs={{4,0},{5,1},{6,2},{7,3},{20,16},{21,17},{22,18},{23,19}} | collective-permute-start | bytes 3145736 | tf_op jit(solution)/shard_map/ppermute | solution.py:452
  83.3 2.8 %collective-permute-start.10 = (bf16[256,1664]{1,0:T(8,128)(2,1)}, bf16[256,1664]{1,0:T(8,128)(2,1)}, u32[]{:S(2)}, u32[]{:S(2)}) collective-permute-start(bf16[256,1664]{1,0:T(8,128)(2,1)} %get-tuple-element.36), channel_id=1, source_target_pairs={{0,1},{1,0},{2,3},{3,2},{4,5},{5,4},{6,7},{7,6},{8,9},{9,8},{10,11... | collective-permute-start | bytes 2555912 | tf_op jit(solution)/shard_map/ppermute | solution.py:477
  83.4 3.9 %collective-permute-start.11 = (bf16[256,1664]{1,0:T(8,128)(2,1)}, bf16[256,1664]{1,0:T(8,128)(2,1)}, u32[]{:S(2)}, u32[]{:S(2)}) collective-permute-start(bf16[256,1664]{1,0:T(8,128)(2,1)} %get-tuple-element.37), channel_id=1, source_target_pairs={{0,1},{1,0},{2,3},{3,2},{4,5},{5,4},{6,7},{7,6},{8,9},{9,8},{10,11... | collective-permute-start | bytes 2555912 | tf_op jit(solution)/shard_map/ppermute | solution.py:477
  97.1 51.8 %collective-permute-start.19 = (bf16[2,256,1664]{2,1,0:T(8,128)(2,1)}, bf16[2,256,1664]{2,1,0:T(8,128)(2,1)}, u32[]{:S(2)}, u32[]{:S(2)}) collective-permute-start(bf16[2,256,1664]{2,1,0:T(8,128)(2,1)} %dot_pair.11.refs_8_), channel_id=1, source_target_pairs={{0,2},{1,3},{2,0},{3,1},{4,6},{5,7},{6,4},{7,5},{8,10},{9,11},{10,... | collective-permute-start | bytes 5111816 | tf_op jit(solution)/shard_map/ppermute | solution.py:484
  113.2 15.0 %collective-permute-start.16 = (bf16[256,1664]{1,0:T(8,128)(2,1)}, bf16[256,1664]{1,0:T(8,128)(2,1)}, u32[]{:S(2)}, u32[]{:S(2)}) collective-permute-start(bf16[256,1664]{1,0:T(8,128)(2,1)} %get-tuple-element.43), channel_id=1, source_target_pairs={{0,1},{1,0},{2,3},{3,2},{4,5},{5,4},{6,7},{7,6},{8,9},{9,8},{10,11... | collective-permute-start | bytes 2555912 | tf_op jit(solution)/shard_map/ppermute | solution.py:477
  113.2 14.9 %collective-permute-start.15 = (bf16[256,1664]{1,0:T(8,128)(2,1)}, bf16[256,1664]{1,0:T(8,128)(2,1)}, u32[]{:S(2)}, u32[]{:S(2)}) collective-permute-start(bf16[256,1664]{1,0:T(8,128)(2,1)} %get-tuple-element.40.refs_7_), channel_id=1, source_target_pairs={{0,1},{1,0},{2,3},{3,2},{4,5},{5,4},{6,7},{7,6},{8,9},{9,8},{10,11... | collective-permute-start | bytes 2555912 | tf_op jit(solution)/shard_map/ppermute | solution.py:477
  127.6 25.2 %collective-permute-start.14 = (bf16[512,1664]{1,0:T(8,128)(2,1)}, bf16[512,1664]{1,0:T(8,128)(2,1)}, u32[]{:S(2)}, u32[]{:S(2)}) collective-permute-start(bf16[512,1664]{1,0:T(8,128)(2,1)} %get-tuple-element.42), channel_id=1, source_target_pairs={{0,1},{1,0},{2,3},{3,2},{4,5},{5,4},{6,7},{7,6},{8,9},{9,8},{10,11... | collective-permute-start | bytes 5111816 | tf_op jit(solution)/shard_map/ppermute | solution.py:477
  127.7 25.0 %collective-permute-start.13 = (bf16[512,1664]{1,0:T(8,128)(2,1)}, bf16[512,1664]{1,0:T(8,128)(2,1)}, u32[]{:S(2)}, u32[]{:S(2)}) collective-permute-start(bf16[512,1664]{1,0:T(8,128)(2,1)} %get-tuple-element.41.refs_7_), channel_id=1, source_target_pairs={{0,1},{1,0},{2,3},{3,2},{4,5},{5,4},{6,7},{7,6},{8,9},{9,8},{10,11... | collective-permute-start | bytes 5111816 | tf_op jit(solution)/shard_map/ppermute | solution.py:477
  137.9 39.5 %collective-permute-start.20 = (bf16[2,256,1664]{2,1,0:T(8,128)(2,1)}, bf16[2,256,1664]{2,1,0:T(8,128)(2,1)}, u32[]{:S(2)}, u32[]{:S(2)}) collective-permute-start(bf16[2,256,1664]{2,1,0:T(8,128)(2,1)} %dot_pair.14.refs_5_), channel_id=1, source_target_pairs={{0,2},{1,3},{2,0},{3,1},{4,6},{5,7},{6,4},{7,5},{8,10},{9,11},{10,... | collective-permute-start | bytes 5111816 | tf_op jit(solution)/shard_map/ppermute | solution.py:484
  148.8 2.8 %collective-permute-start.17 = (bf16[256,1664]{1,0:T(8,128)(2,1)}, bf16[256,1664]{1,0:T(8,128)(2,1)}, u32[]{:S(2)}, u32[]{:S(2)}) collective-permute-start(bf16[256,1664]{1,0:T(8,128)(2,1)} %get-tuple-element.44), channel_id=1, source_target_pairs={{0,1},{1,0},{2,3},{3,2},{4,5},{5,4},{6,7},{7,6},{8,9},{9,8},{10,11... | collective-permute-start | bytes 2555912 | tf_op jit(solution)/shard_map/ppermute | solution.py:477
  148.9 3.9 %collective-permute-start.18 = (bf16[256,1664]{1,0:T(8,128)(2,1)}, bf16[256,1664]{1,0:T(8,128)(2,1)}, u32[]{:S(2)}, u32[]{:S(2)}) collective-permute-start(bf16[256,1664]{1,0:T(8,128)(2,1)} %get-tuple-element.45), channel_id=1, source_target_pairs={{0,1},{1,0},{2,3},{3,2},{4,5},{5,4},{6,7},{7,6},{8,9},{9,8},{10,11... | collective-permute-start | bytes 2555912 | tf_op jit(solution)/shard_map/ppermute | solution.py:477
  177.5 9.9 %copy-start.1 = (f32[8,2,6656]{2,1,0:T(2,128)S(1)}, f32[8,2,6656]{2,1,0:T(2,128)}, u32[]{:S(2)}) copy-start(f32[8,2,6656]{2,1,0:T(2,128)} %param.14) | copy-start | bytes 1277956
